TPU v7x, 512 devices: a whole 4x8x8 slice. The times are simulated.
512 devices in a mesh: section: 2 (over y_hi), dp: 64 (over y_lo, z, core), tp: 4 (over x).
Axes of the slice: x: 4, y: 8 (y_hi: 2, y_lo: 4; y = y_hi * 4 + y_lo), z: 8, core: 2. Of those that a mesh axis runs over, the one named last changes fastest.
Arguments:
- cache: bfloat16 [128, 96, 64, 576], P(('section', 'dp'), 'tp'), may hold values from -6 to 6
- sent: bfloat16 [128, 16, 64, 576], P(('section', 'dp'), 'tp'), may hold values from -6 to 6
- slot_of: int32 [128, 16], P(('section', 'dp'), 'tp'), may hold values from 0 to 23, as said below
- table: int32 [128, 96], P(('section', 'dp'), 'tp'), may hold values from 0 to 95, each once within a row
- lengths: int32 [128], P(('section', 'dp')), may hold values from 64 to 6144
- new_kv: bfloat16 [128, 2, 576], P(('section', 'dp')), may hold values from -6 to 6
- queries: bfloat16 [128, 2, 64, 576], P(('section', 'dp')), may hold values from -24 to 24
- resid: bfloat16 [128, 2, 7168], P(('section', 'dp'), None, 'tp'), may hold values from -6 to 6
- gain: float32 [7168], P('tp'), may hold values from 0.25 to 1.75
- w_ov: bfloat16 [32768, 7168], P(('section', 'dp'), 'tp'), may hold values from -0.25 to 0.25
- w_gate: bfloat16 [7168, 18432], P('tp', ('section', 'dp')), may hold values from -0.0625 to 0.0625
- w_up: bfloat16 [7168, 18432], P('tp', ('section', 'dp')), may hold values from -0.0625 to 0.0625
- w_down: bfloat16 [18432, 7168], P(('section', 'dp'), 'tp'), may hold values from -0.046875 to 0.046875
Outputs:
- output: bfloat16 [128, 2, 7168], P(('section', 'dp'), None, 'tp')
Inputs may be any that keep to these rules, and one draw needn't show every extreme that they name: `slot_of`: within each row, the 4 entries that belong to one device of tp name different slots.
All inputs are finite; a program needn't handle non-finite values.
Results may differ from a plain program's by a relative error of at most 0.011.
Values may be sent and summed in bfloat16 or wider, within the bound.
A program may use at most 128 MiB of HBM per device.

v0:
```python
import jax
import jax.numpy as jnp
from jax import lax
from jax.sharding import PartitionSpec as P

D = 7168
LAT = 512


SCALE = 192.0 ** (-0.5)
EPS = 1e-06


def partner(value, axis, stride):
    mask = 2**stride
    pairs = [(source, source ^ mask) for source in range(lax.axis_size(axis))]
    return lax.ppermute(value, axis, pairs)


def joined(x, axis, combine):
    everything = jax.tree.map(lambda part: lax.all_gather(part, axis), x)
    first = jax.tree.map(lambda part: part[0], everything)

    def step(k, so_far):
        return combine(so_far, jax.tree.map(lambda part: part[k], everything))

    return lax.fori_loop(1, lax.axis_size(axis), step, first)


def page_attention(queries, page_rows, usable):
    row_count, slot_count, page_len, entry = page_rows.shape
    flat_keys = page_rows.reshape(row_count, slot_count * page_len, entry)
    scores = (
        jnp.einsum("rphk,rnk->rphn", queries, flat_keys, preferred_element_type=jnp.float32) * SCALE
    )
    scores = jnp.where(usable.reshape(row_count, 1, 1, slot_count * page_len), scores, -jnp.inf)
    top_score = jnp.maximum(jnp.max(scores, axis=-1), -1e30)
    weights = jnp.exp(scores - top_score[..., None])
    prob_sum = jnp.sum(weights, axis=-1)
    weighted = jnp.einsum(
        "rphn,rnl->rphl",
        weights.astype(jnp.bfloat16),
        flat_keys[:, :, :LAT],
        preferred_element_type=jnp.float32,
    )
    return (top_score, prob_sum, weighted)


def combine(earlier, later):
    top_score = jnp.maximum(earlier[0], later[0])
    scale_one = jnp.exp(earlier[0] - top_score)
    scale_two = jnp.exp(later[0] - top_score)
    prob_sum = earlier[1] * scale_one + later[1] * scale_two
    weighted = earlier[2] * scale_one[..., None] + later[2] * scale_two[..., None]
    return (top_score, prob_sum, weighted)


def body(
    cache, sent, slot_of, table, lengths, new_kv, queries, resid, gain, w_ov, w_gate, w_up, w_down
):
    row_count, slot_count, page_len, entry = cache.shape
    received = partner(sent, "section", 0)
    offsets = jnp.arange(page_len, dtype=jnp.int32)
    position = table[:, :, None] * page_len + offsets[None, None, :]
    usable = position < lengths[:, None, None]
    filled = jax.vmap(lambda page_rows, targets, incoming: page_rows.at[targets].set(incoming))(
        cache, slot_of, received
    )
    partial_soft = page_attention(queries, filled, usable)
    top_score, prob_sum, weighted = joined(partial_soft, "tp", combine)
    extra = (
        jnp.einsum("rphk,rek->rphe", queries, new_kv, preferred_element_type=jnp.float32) * SCALE
    )
    causal = jnp.arange(2, dtype=jnp.int32)[:, None] >= jnp.arange(2, dtype=jnp.int32)[None, :]
    extra = jnp.where(causal[None, :, None, :], extra, -jnp.inf)
    summit = jnp.maximum(top_score, jnp.max(extra, axis=-1))
    shrink = jnp.exp(top_score - summit)
    extra_weights = jnp.exp(extra - summit[..., None])
    prob_sum = prob_sum * shrink + jnp.sum(extra_weights, axis=-1)
    weighted = weighted * shrink[..., None] + jnp.einsum(
        "rphe,rel->rphl",
        extra_weights.astype(jnp.bfloat16),
        new_kv[:, :, :LAT],
        preferred_element_type=jnp.float32,
    )
    latent = (weighted / prob_sum[..., None]).astype(jnp.bfloat16)
    flat = latent.reshape(row_count, 2, -1)
    regrouped = lax.all_to_all(flat, ("section", "dp"), split_axis=2, concat_axis=0, tiled=True)
    everyone = regrouped.shape[0]
    partial_value = jnp.dot(
        regrouped.reshape(everyone * 2, -1), w_ov, preferred_element_type=jnp.float32
    ).reshape(everyone, 2, -1)
    feature_count = partial_value.shape[2]
    group = lax.axis_index(("section", "dp"))
    row_start = group * row_count
    own_rows = lax.dynamic_slice_in_dim(partial_value, row_start, row_count, 0) + resid.astype(
        jnp.float32
    )
    partial_value = lax.dynamic_update_slice_in_dim(partial_value, own_rows, row_start, 0)
    resid_sum = lax.psum(partial_value, ("section", "dp"))
    normed = (resid_sum * gain).astype(jnp.bfloat16).reshape(everyone * 2, feature_count)
    gate_part = jnp.dot(normed, w_gate, preferred_element_type=jnp.float32)
    up_part = jnp.dot(normed, w_up, preferred_element_type=jnp.float32)
    row_squares = jnp.sum(resid_sum * resid_sum, axis=-1)
    gate_sum, up_sum, squares = (
        lax.psum(gate_part.astype(jnp.bfloat16), "tp").astype(jnp.float32),
        lax.psum(up_part.astype(jnp.bfloat16), "tp").astype(jnp.float32),
        lax.psum(row_squares.astype(jnp.bfloat16), "tp").astype(jnp.float32),
    )
    base_rows = lax.dynamic_slice_in_dim(resid_sum, row_start, row_count, 0)
    factor = lax.rsqrt(squares.reshape(everyone * 2, 1) / D + EPS)
    hidden = (jax.nn.silu(gate_sum * factor) * (up_sum * factor)).astype(jnp.bfloat16)
    hidden = hidden.reshape(everyone, 2, -1)
    term = jnp.einsum("rpf,fd->rpd", hidden, w_down, preferred_element_type=jnp.float32)
    projected = lax.psum_scatter(term, ("section", "dp"), scatter_dimension=0, tiled=True)
    return (base_rows + projected).astype(jnp.bfloat16)


def solution(mesh):
    in_specs = (
        P(("section", "dp"), "tp", None, None),
        P(("section", "dp"), "tp", None, None),
        P(("section", "dp"), "tp"),
        P(("section", "dp"), "tp"),
        P(("section", "dp")),
        P(("section", "dp"), None, None),
        P(("section", "dp"), None, None, None),
        P(("section", "dp"), None, "tp"),
        P("tp"),
        P(("section", "dp"), "tp"),
        P("tp", ("section", "dp")),
        P("tp", ("section", "dp")),
        P(("section", "dp"), "tp"),
    )
    out_specs = P(("section", "dp"), None, "tp")
    return jax.shard_map(body, mesh=mesh, in_specs=in_specs, out_specs=out_specs, check_vma=False)
```

profile of v0, /device:TPU:1, one launch (start us, length us, event | category | flops | bytes accessed | tf_op | source)
XLA Modules:
  0.0 853.2 jit_solution(17107962758501848223)
XLA Ops:
  6.6 8.5 %collective-permute-start = (bf16[1,4,64,576]{3,2,1,0:T(8,128)(2,1)}, bf16[1,4,64,576]{3,2,1,0:T(8,128)(2,1)S(1)}, u32[]{:S(2)}, u32[]{:S(2)}) collective-permute-start(bf16[1,4,64,576]{3,2,1,0:T(8,128)(2,1)} %param.16), channel_id=1, source_target_pairs={{0,256},{256,0},{1,257},{257,1},{2,258},{258,2},{3,259},{259,3},{4... | collective-permute-start | bytes 884744 | tf_op jit(solution)/shard_map/ppermute | solution.py:17
  16.1 8.5 collective-permute-done
  27.1 1.1 fusion.7
  28.5 1.4 fusion.15
  29.9 7.4 all-gather.4
  37.3 5.2 all-gather.3
  42.6 24.4 %all-gather.7.cloned.1.call-done = f32[8,64,512]{2,1,0:T(8,128)} async-done(((f32[2,64,512]{2,1,0:T(8,128)}), f32[8,64,512]{2,1,0:T(8,128)}) %all-gather.7.cloned.1.call-update) | async-done | bytes 1048592 | tf_op jit(solution)/shard_map/all_gather | solution.py:21
  67.0 1.0 slice_bitcast_fusion.2
  68.0 3.5 while.19
  68.0 1.1 fusion.50
  69.2 1.1 fusion.50
  70.3 1.1 fusion.50
  71.8 25.5 %copy.48 = bf16[1,2,32768]{1,0,2:T(2,128)(2,1)} copy(bf16[1,2,32768]{2,1,0:T(2,128)(2,1)S(1)} %reshape.194) | data formatting | bytes 262144 | tf_op jit(solution)/shard_map/reshape | solution.py:87
  97.9 179.1 %reduce.12 = bf16[32768,2]{1,0:T(8,128)(2,1)} reduce(bf16[32768,1,2]{2,1,0:T(2,128)(2,1)} %bitcast.140, bf16[]{:T(256)} %broadcast.120), dimensions={1}, to_apply=%bitcast.117.reduce_sub_computation | reduce | bytes 262146
  277.0 13.7 %reshape.244 = bf16[128,2,256]{2,1,0:T(2,128)(2,1)} reshape(bf16[32768,2]{1,0:T(8,128)(2,1)} %reduce.12) | data formatting | bytes 262144
  290.7 15.2 %all-to-all-start = ((bf16[128,2,256]{2,1,0:T(2,128)(2,1)}), bf16[128,2,256]{2,1,0:T(2,128)(2,1)S(1)}, u32[]{:S(2)}, u32[]{:S(2)}) async-start(bf16[128,2,256]{2,1,0:T(2,128)(2,1)} %reshape.244), calls=%async_computation | async-start | bytes 262144 | tf_op jit(solution)/shard_map/all_to_all | solution.py:88
  305.9 12.1 %all-to-all-done = bf16[128,2,256]{2,1,0:T(2,128)(2,1)S(1)} async-done(((bf16[128,2,256]{2,1,0:T(2,128)(2,1)}), bf16[128,2,256]{2,1,0:T(2,128)(2,1)S(1)}, u32[]{:S(2)}, u32[]{:S(2)}) %all-to-all-start) | async-done | bytes 131104 | tf_op jit(solution)/shard_map/all_to_all | solution.py:88
  318.1 32.6 %reshape.245 = bf16[32768,1,2]{2,1,0:T(2,128)(2,1)} reshape(bf16[128,2,256]{2,1,0:T(2,128)(2,1)S(1)} %all-to-all-done) | data formatting | bytes 262144
  350.7 30.6 %copy.49 = bf16[1,2,32768]{2,1,0:T(2,128)(2,1)S(1)} copy(bf16[1,2,32768]{1,0,2:T(2,128)(2,1)} %bitcast.141) | data formatting | bytes 262144 | tf_op jit(solution)/shard_map/all_to_all | solution.py:88
  381.7 1.4 copy.51
  383.2 1.2 copy-done.1
  384.5 191.2 %all-reduce.6.cloned.1.call-done = f32[128,2,1792]{2,1,0:T(2,128)} async-done(((f32[128,2,1792]{2,1,0:T(2,128)}), f32[128,2,1792]{2,1,0:T(2,128)}) %all-reduce.6.cloned.1.call-update) | async-done | bytes 1835024 | tf_op jit(solution)/shard_map/psum | solution.py:100
  575.7 2.8 multiply_reduce_fusion
  578.9 1.1 convolution_convert_fusion
  580.0 2.1 convolution_convert_fusion.1
  582.2 8.4 psum.30
  590.9 47.5 %all-reduce.10.cloned.1.call-done = (bf16[256,144]{0,1:T(8,128)(2,1)}, bf16[256,144]{0,1:T(8,128)(2,1)}) async-done(((bf16[256,144]{0,1:T(8,128)(2,1)}, bf16[256,144]{0,1:T(8,128)(2,1)}), (bf16[256,144]{0,1:T(8,128)(2,1)}, bf16[256,144]{0,1:T(8,128)(2,1)})) %all-reduce.10.cloned.1.call-update) | async-done | bytes 147472 | tf_op jit(solution)/shard_map/psum | solution.py:107
  638.4 1.0 multiply_convert_fusion.1
  640.0 2.7 copy.56
  642.7 1.3 dynamic-slice
  644.0 200.7 %all-reduce.8.cloned.1.call-done = f32[128,2,1792]{2,1,0:T(2,128)} async-done(((f32[128,2,1792]{2,1,0:T(2,128)}), f32[128,2,1792]{2,1,0:T(2,128)}) %all-reduce.8.cloned.1.call-update) | async-done | bytes 1835024
  844.7 2.0 fusion.24
  (72 shorter events, 5.9 us)
Async XLA Ops:
  6.5 374.7 %copy-start = (bf16[256,1792]{1,0:T(8,128)(2,1)S(1)}, bf16[256,1792]{1,0:T(8,128)(2,1)}, u32[]{:S(2)}) copy-start(bf16[256,1792]{1,0:T(8,128)(2,1)} %param.24) | copy-start | bytes 2752516
  6.5 18.1 %copy-start.2 = (bf16[1,24,64,576]{3,2,1,0:T(8,128)(2,1)S(1)}, bf16[1,24,64,576]{3,2,1,0:T(8,128)(2,1)}, u32[]{:S(2)}) copy-start(bf16[1,24,64,576]{3,2,1,0:T(8,128)(2,1)} %param.15) | copy-start | bytes 5308420
  6.5 8.6 %copy-start.10 = (s32[1,4]{1,0:T(1,128)S(1)}, s32[1,4]{1,0:T(1,128)}, u32[]{:S(2)}) copy-start(s32[1,4]{1,0:T(1,128)} %param.17) | copy-start | bytes 52
  6.5 8.7 %copy-start.11 = (s32[1,24]{1,0:T(1,128)S(1)}, s32[1,24]{1,0:T(1,128)}, u32[]{:S(2)}) copy-start(s32[1,24]{1,0:T(1,128)} %param.18) | copy-start | bytes 292
  6.5 18.8 %copy-start.8 = (bf16[1,2,64,576]{3,2,1,0:T(8,128)(2,1)S(1)}, bf16[1,2,64,576]{3,2,1,0:T(8,128)(2,1)}, u32[]{:S(2)}) copy-start(bf16[1,2,64,576]{3,2,1,0:T(8,128)(2,1)} %param.21) | copy-start | bytes 442372
  6.5 60.5 %all-gather.7.cloned.1.call-start = ((), (), s32[]{:S(2)}) async-start(), calls=%async_computation.2 | async-start | bytes 1310720 | tf_op jit(solution)/shard_map/all_gather | solution.py:21
  6.6 18.1 %collective-permute-start = (bf16[1,4,64,576]{3,2,1,0:T(8,128)(2,1)}, bf16[1,4,64,576]{3,2,1,0:T(8,128)(2,1)S(1)}, u32[]{:S(2)}, u32[]{:S(2)}) collective-permute-start(bf16[1,4,64,576]{3,2,1,0:T(8,128)(2,1)} %param.16), channel_id=1, source_target_pairs={{0,256},{256,0},{1,257},{257,1},{2,258},{258,2},{3,259},{259,3},{4... | collective-permute-start | bytes 884744 | tf_op jit(solution)/shard_map/ppermute | solution.py:17
  26.2 0.9 copy-start.3
  26.2 2.1 copy-start.9
  290.7 27.4 %all-to-all-start = ((bf16[128,2,256]{2,1,0:T(2,128)(2,1)}), bf16[128,2,256]{2,1,0:T(2,128)(2,1)S(1)}, u32[]{:S(2)}, u32[]{:S(2)}) async-start(bf16[128,2,256]{2,1,0:T(2,128)(2,1)} %reshape.244), calls=%async_computation | async-start | bytes 262144 | tf_op jit(solution)/shard_map/all_to_all | solution.py:88
  305.9 269.8 %all-reduce.6.cloned.1.call-start = ((), (), s32[]{:S(2)}) async-start(), calls=%async_computation.1 | async-start | bytes 3670016 | tf_op jit(solution)/shard_map/psum | solution.py:100
  381.7 1.4 copy-start.7
  383.1 192.6 %copy-start.6 = (f32[1792]{0:T(1024)S(1)}, f32[1792]{0:T(1024)}, u32[]{:S(2)}) copy-start(f32[1792]{0:T(1024)} %param.23) | copy-start | bytes 21508
  383.1 1.2 copy-start.1
  384.4 194.5 %copy-start.4 = (bf16[1792,144]{0,1:T(8,128)(2,1)S(1)}, bf16[1792,144]{0,1:T(8,128)(2,1)}, u32[]{:S(2)}) copy-start(bf16[1792,144]{0,1:T(8,128)(2,1)} %param.26) | copy-start | bytes 1548292
  384.4 254.0 %all-reduce.10.cloned.1.call-start = ((), (), s32[]{:S(2)}) async-start(), calls=%async_computation.4 | async-start | bytes 294912 | tf_op jit(solution)/shard_map/psum | solution.py:107
  578.9 60.7 %copy-start.5 = (bf16[144,1792]{1,0:T(8,128)(2,1)S(1)}, bf16[144,1792]{1,0:T(8,128)(2,1)}, u32[]{:S(2)}) copy-start(bf16[144,1792]{1,0:T(8,128)(2,1)} %param.27) | copy-start | bytes 1548292
  590.6 254.1 %all-reduce.8.cloned.1.call-start = ((), (), s32[]{:S(2)}) async-start(), calls=%async_computation.3 | async-start | bytes 3670016
Sparse Core Ops, SparseCore 0:
  28.4 38.5 all-gather.6
  384.5 191.1 all-reduce.5
  590.7 47.6 all-reduce.9
  642.8 201.8 all-reduce.7
where the time goes:
time: 855 us; the launch traced here: 853 us
  waiting for transfers between devices  485 us (57%)
  other arithmetic  190 us (22%)
  local copies, waits for them, and re-layouts  113 us (13%)
  starting transfers between devices  23.9 us (3%)
  blocking collectives  21 us (2%)
  between operations  14.1 us (2%)
    unnamed x5, waiting for transfers between devices  201 us
    psum x1, waiting for transfers between devices, body(): resid_sum = lax.psum(partial_value, ('section', 'dp'))  191 us
    unnamed x1, other arithmetic  179 us
    unnamed x29, local copies, waits for them, and re-layouts  50.3 us
    psum x1, waiting for transfers between devices, body(): lax.psum(up_part.astype(jnp.bfloat16), 'tp').astype(jnp.float32)  47.5 us
    all_to_all x1, local copies, waits for them, and re-layouts, body(): lax.all_to_all(flat, ('section', 'dp'), split_axis=2, concat_axis=0, tile...  30.6 us
    reshape x2, local copies, waits for them, and re-layouts, body(): flat = latent.reshape(row_count, 2, -1)  25.6 us
    all_gather x1, waiting for transfers between devices, joined(): everything = jax.tree.map(lambda part: lax.all_gather(part, axis), x)  24.4 us
  transfers between devices with their start and end apart: 6, of which 6 were waited for; matrix products, arithmetic and copies ran while one was open for 0% of the time, Pallas kernels for 0%

commit v1 on v0

v1 whole, which is shorter than its diff:
```python
import functools

import jax
import jax.numpy as jnp
from jax import lax
from jax.experimental import pallas as pl
from jax.experimental.pallas import tpu as pltpu
from jax.sharding import PartitionSpec as P

D = 7168
LAT = 512
SCALE = 192.0 ** (-0.5)
EPS = 1e-06
LOW = -1e30
FLOOR = -1e20
MESH = pl.DeviceIdType.MESH
BF = jnp.bfloat16
F32 = jnp.float32
HALF = 896
PAIRS = 7

NT = (((1,), (1,)), ((), ()))


def dot(a, b):
    return jnp.dot(a, b, preferred_element_type=F32)


def swap_rows(x, scratch):
    blocks = x.shape[1] // 128
    for c in range(2):
        for a in range(8):
            for p in range(2):
                row = c * 128 + a * 16 + p * 8
                for n in range(blocks):
                    scratch[n, pl.ds(c * 128 + p * 8 + a, 8, stride=16), :] = x[
                        row : row + 8, n * 128 : (n + 1) * 128
                    ]
    return jnp.concatenate([scratch[n] for n in range(blocks)], axis=1)


def kernel(
    lengths_ref,
    table_ref,
    slot_ref,
    new_ref,
    resid_ref,
    gain_ref,
    cache_ref,
    sent_ref,
    query_ref,
    wov_ref,
    wgate_ref,
    wup_ref,
    wdown_ref,
    out_ref,
    kv,
    kx,
    kn,
    qs,
    wov,
    wg,
    wu,
    wc,
    wd,
    xs_send,
    xs_recv,
    lat,
    l1,
    tf,
    tb,
    a1,
    a2,
    perm,
    core_send,
    core_recv,
    tot,
    send1,
    recv1,
    pack,
    send2,
    recv2,
    rsd,
    gpk,
    recv3,
    unp,
    n0,
    n1,
    gs,
    recvx,
    hid,
    flat,
    load_sem,
    hand_sem,
    xs_ss,
    xs_rs,
    ly_ss,
    ly_rs,
    lx_ss,
    lx_rs,
    lz_ss,
    lz_rs,
    core_ss,
    core_rs,
    p1_ss,
    p1_rs,
    p2_ss,
    p2_rs,
    p3_ss,
    p3_rs,
    p4_ss,
    p4_rs,
    p5_ss,
    p5_rs,
    gx_ss,
    gx_rs,
    hx_ss,
    hx_rs,
):
    dp = lax.axis_index("dp")
    t = lax.axis_index("tp")
    Y = lax.axis_index("section") * 4 + dp // 16
    zc = dp % 16
    z = zc // 2
    c = zc % 2
    sib = 1 - c

    def dev(y_, zc_, t_):
        return (y_ // 4, (y_ % 4) * 16 + zc_, t_)

    def along(s, first, k):
        if (s == 0) == first:
            return dev(Y, ((z + k) % 8) * 2 + c, t)
        return dev((Y + k) % 8, zc, t)

    here = (z, Y)
    there = (Y, z)
    sibling = dev(Y, z * 2 + sib, t)

    def remote(src, dst, ss, rs, to):
        return pltpu.make_async_remote_copy(
            src_ref=src, dst_ref=dst, send_sem=ss, recv_sem=rs, device_id=to, device_id_type=MESH
        )

    def landed(region, ss, rs):
        remote(region, region, ss, rs, sibling).wait_recv()

    loads = [
        pltpu.make_async_copy(cache_ref.at[0], kv, load_sem.at[0]),
        pltpu.make_async_copy(query_ref.at[0], qs, load_sem.at[1]),
        pltpu.make_async_copy(wov_ref, wov, load_sem.at[2]),
        pltpu.make_async_copy(wgate_ref, wg, load_sem.at[3]),
        pltpu.make_async_copy(wup_ref, wu, load_sem.at[4]),
        pltpu.make_async_copy(wdown_ref, wd.at[pl.ds(0, 144)], load_sem.at[5]),
    ]
    for load in loads:
        load.start()

    barrier = pltpu.get_barrier_semaphore()
    for k in range(1, 8):
        pl.semaphore_signal(barrier, inc=1, device_id=dev((Y + k) % 8, zc, t), device_id_type=MESH)
    for k in range(1, 16):
        pl.semaphore_signal(barrier, inc=1, device_id=dev(Y, (zc + k) % 16, t), device_id_type=MESH)
    for k in range(1, 4):
        pl.semaphore_signal(barrier, inc=1, device_id=dev(Y, zc, (t + k) % 4), device_id_type=MESH)
    pl.semaphore_wait(barrier, 25)

    hand = remote(sent_ref.at[0], kx, hand_sem.at[0], hand_sem.at[1], dev((Y + 4) % 8, zc, t))
    hand.start()

    resid = resid_ref[0].astype(F32)
    for s in range(2):
        rsd[s] = jnp.zeros((16, 128), F32)
        gpk[s] = jnp.zeros((16, 128), F32)
        for p in range(2):
            for k in range(PAIRS):
                n = s * PAIRS + k
                rsd[s, p * 8 + k : p * 8 + k + 1, :] = resid[p : p + 1, n * 128 : (n + 1) * 128]
                gpk[s, p * 8 + k : p * 8 + k + 1, :] = gain_ref[0:1, n * 128 : (n + 1) * 128]
    wd[pl.ds(144, 112)] = jnp.zeros((112, 1792), BF)
    kn[...] = jnp.zeros((128, 576), BF)
    kn[0:2, :] = new_ref[0]

    loads[3].wait()
    loads[4].wait()
    for r in range(0, 1792, 256):
        rows = pl.ds(r, 256)
        gate_w = wg[rows]
        up_w = wu[rows]
        wc[rows, 0:128] = gate_w[:, 0:128]
        wc[rows, 128:256] = up_w[:, 0:128]
        wc[rows, 256:384] = jnp.concatenate(
            [
                gate_w[:, 128:144].astype(F32),
                up_w[:, 128:144].astype(F32),
                jnp.zeros((256, 96), F32),
            ],
            axis=1,
        ).astype(BF)

    lane = lax.broadcasted_iota(jnp.int32, (1, 128), 1)
    inside = lane % 64
    length = lengths_ref[0]

    def bias_of(first, second):
        return jnp.where(inside < jnp.where(lane < 64, first, second), 0.0, LOW)

    limits = []
    for slot in range(24):
        limit = length - table_ref[0, slot] * 64
        for e in range(4):
            limit = jnp.where(slot_ref[0, e] == slot, 0, limit)
        limits.append(limit)
    bias = jnp.concatenate([bias_of(limits[i], limits[i + 1]) for i in range(0, 24, 2)], axis=1)
    late = [length - table_ref[0, slot_ref[0, e]] * 64 for e in range(4)]
    bias_x = jnp.concatenate([bias_of(late[0], late[1]), bias_of(late[2], late[3])], axis=1)
    head = lax.broadcasted_iota(jnp.int32, (128, 128), 0)
    entry = lax.broadcasted_iota(jnp.int32, (128, 128), 1)
    fresh = jnp.where(t == 0, 1, 0)
    bias_n = jnp.where(entry < jnp.where(head < 64, 1, 2) * fresh, 0.0, LOW)

    loads[0].wait()
    loads[1].wait()
    q = qs[...].reshape(128, 576)
    keys = kv[...].reshape(1536, 576)
    scores = lax.dot_general(q, keys, NT, preferred_element_type=F32) * SCALE + bias
    scores_n = lax.dot_general(q, kn[...], NT, preferred_element_type=F32) * SCALE + bias_n
    top = jnp.maximum(
        jnp.max(scores, axis=1, keepdims=True), jnp.max(scores_n, axis=1, keepdims=True)
    )
    top = jnp.maximum(top, FLOOR)
    w = jnp.exp(scores - top)
    w_n = jnp.exp(scores_n - top)
    total = jnp.sum(w, axis=1, keepdims=True) + jnp.sum(w_n, axis=1, keepdims=True)
    acc = dot(w.astype(BF), keys[:, :LAT]) + dot(w_n.astype(BF), kn[:, :LAT])

    hand.wait_recv()
    keys = kx[...].reshape(256, 576)
    scores = lax.dot_general(q, keys, NT, preferred_element_type=F32) * SCALE + bias_x
    top_all = jnp.maximum(top, jnp.max(scores, axis=1, keepdims=True))
    w = jnp.exp(scores - top_all)
    shrink = jnp.exp(top - top_all)
    total = total * shrink + jnp.sum(w, axis=1, keepdims=True)
    acc = acc * shrink + dot(w.astype(BF), keys[:, :LAT])
    total = jnp.where(total > 0.0, total, 1.0)
    acc = acc / total
    lse = top_all + jnp.log(total)
    hi = lse.astype(BF).astype(F32)
    mid = (lse - hi).astype(BF).astype(F32)
    low = lse - hi - mid
    tail = jnp.where(entry < 32, hi, jnp.where(entry < 64, mid, low))
    for n in range(4):
        flat[n] = acc[:, n * 128 : (n + 1) * 128]
    flat[4] = tail

    def part_of(dest, j):
        block = (Y + dest + 4 * j) % 8
        rows = []
        for p in range(2):
            at = pl.ds(pl.multiple_of(p * 64 + block * 8, 8), 8)
            rows.append(jnp.concatenate([flat[n, at, :] for n in range(5)], axis=1))
        return jnp.concatenate(rows, axis=0)

    xs = []
    for k in range(1, 4):
        to = (t + k) % 4
        for j in range(2):
            xs_send[k, j] = part_of(to, j).astype(BF)
        copy = remote(xs_send.at[k], xs_recv.at[k], xs_ss.at[k], xs_rs.at[k], dev(Y, zc, to))
        copy.start()
        xs.append(copy)
    mine = [part_of(t, j) for j in range(2)]
    for copy in xs:
        copy.wait_recv()
    for j in range(2):
        parts = [mine[j]] + [xs_recv[k, j].astype(F32) for k in range(1, 4)]
        lses = [part[:, 512:513] + part[:, 544:545] + part[:, 576:577] for part in parts]
        best = functools.reduce(jnp.maximum, lses)
        shares = [jnp.exp(value - best) for value in lses]
        norm = functools.reduce(jnp.add, shares)
        mixed = functools.reduce(
            jnp.add, [part[:, :LAT] * share for part, share in zip(parts, shares)]
        )
        lat[j] = (mixed / norm).astype(BF)

    ly = [
        remote(
            lat.at[j], l1.at[t * 2 + j], ly_ss.at[j], ly_rs.at[j], dev((Y + t + 4 * j) % 8, zc, t)
        )
        for j in range(2)
    ]
    ly[1].start()

    @pl.when(t != 0)
    def _():
        ly[0].start()

    @pl.when(t == 0)
    def _():
        l1[0] = lat[0]

    for copy in xs:
        copy.wait_send()

    @pl.when(t != 0)
    def _():
        ly[0].wait_recv()

    ly[1].wait_recv()
    lx = []
    own = l1.at[pl.ds(t * 2, 2)]
    for k in range(1, 4):
        copy = remote(own, own, lx_ss.at[k], lx_rs.at[k], dev(Y, zc, (t + k) % 4))
        copy.start()
        lx.append(copy)
    ly[1].wait_send()

    @pl.when(t != 0)
    def _():
        ly[0].wait_send()

    for k in range(4):
        source = (t - k + 4) % 4
        if k:
            landed(l1.at[pl.ds(source * 2, 2)], lx_ss.at[k], lx_rs.at[k])
        for j in range(2):
            block = l1[source * 2 + j].astype(F32)
            y_from = (Y - source - 4 * j + 8) % 8
            for p in range(2):
                for n in range(4):
                    tf[n, pl.ds(p * 8 + y_from, 8, stride=16), :] = block[
                        p * 8 : p * 8 + 8, n * 128 : (n + 1) * 128
                    ]
    for n in range(2):
        tb[n] = jnp.concatenate([tf[2 * n], tf[2 * n + 1]], axis=1).astype(BF)
    lz = []

    def a_rows(zc_):
        return pl.ds(pl.multiple_of(((zc_ % 2) * 8 + zc_ // 2) * 16, 16), 16)

    for k in range(1, 16):
        to = (zc + k) % 16
        copy = remote(
            tb.at[to % 2, pl.ds(pl.multiple_of((to // 2) * 16, 16), 16)],
            a1.at[a_rows(zc)],
            lz_ss.at[k],
            lz_rs.at[k],
            dev(Y, to, t),
        )
        copy.start()
        lz.append(copy)
    a1[a_rows(zc), :] = tb[c, pl.ds(pl.multiple_of(z * 16, 16), 16), :]
    for copy in lx:
        copy.wait_send()
    loads[2].wait()
    loads[5].wait()
    for k in range(1, 16):
        landed(a1.at[a_rows((zc - k + 16) % 16)], lz_ss.at[k], lz_rs.at[k])
    wide = a1[...].astype(F32)
    a2[...] = swap_rows(wide, perm).astype(BF)
    for copy in lz:
        copy.wait_send()

    def reduced(u, operands, weight):
        started = []
        ours = []
        for s in range(2):
            columns = slice(s * HALF, (s + 1) * HALF)
            rows = pl.ds(pl.multiple_of(sib * 128, 128), 128)
            core_send[u, s] = dot(operands[s][rows, :], weight[:, columns]).astype(BF)
            copy = remote(
                core_send.at[u, s],
                core_recv.at[u, s],
                core_ss.at[u, s],
                core_rs.at[u, s],
                sibling,
            )
            copy.start()
            started.append(copy)
        for s in range(2):
            columns = slice(s * HALF, (s + 1) * HALF)
            rows = pl.ds(pl.multiple_of(c * 128, 128), 128)
            tot[s] = dot(operands[s][rows, :], weight[:, columns])
        first = []
        for s in range(2):
            started[s].wait_recv()
            tot[s] = tot[s] + core_recv[u, s].astype(F32)
            send1[u, s] = tot[s].astype(BF)
            copies = []
            for k in range(1, 8):
                block = (here[s] + k) % 8
                copy = remote(
                    send1.at[u, s, pl.ds(pl.multiple_of(block * 16, 16), 16)],
                    recv1.at[u, s, k],
                    p1_ss.at[u, s, k],
                    p1_rs.at[u, s, k],
                    along(s, True, k),
                )
                copy.start()
                copies.append(copy)
            first.append(copies)
        for copy in started:
            copy.wait_send()
        second = []
        for s in range(2):
            part = tot[s, pl.ds(pl.multiple_of(here[s] * 16, 16), 16), :]
            for k in range(1, 8):
                first[s][k - 1].wait_recv()
                part = part + recv1[u, s, k].astype(F32)
            for p in range(2):
                for k in range(PAIRS):
                    pack[s, pl.ds(p * 8 + k, 8, stride=16), :] = part[
                        p * 8 : p * 8 + 8, k * 128 : (k + 1) * 128
                    ]
                pack[s, pl.ds(p * 8 + PAIRS, 8, stride=16), :] = jnp.zeros((8, 128), F32)
            send2[u, s] = pack[s].astype(BF)
            copies = []
            for k in range(1, 8):
                block = (there[s] + k) % 8
                copy = remote(
                    send2.at[u, s, pl.ds(pl.multiple_of(block * 16, 16), 16)],
                    recv2.at[u, s, k],
                    p2_ss.at[u, s, k],
                    p2_rs.at[u, s, k],
                    along(s, False, k),
                )
                copy.start()
                copies.append(copy)
            second.append(copies)
        for copies in first:
            for copy in copies:
                copy.wait_send()
        result = []
        for s in range(2):
            part = pack[s, pl.ds(pl.multiple_of(there[s] * 16, 16), 16), :]
            for k in range(1, 8):
                second[s][k - 1].wait_recv()
                part = part + recv2[u, s, k].astype(F32)
            result.append(part)
        return result, [copy for copies in second for copy in copies]

    attended, pending = reduced(0, (a1, a2), wov)

    sums = []
    squares = []
    for s in range(2):
        value = attended[s] + rsd[s]
        rsd[s] = value
        sums.append(value)
        squares.append(value * value)
    both = squares[0] + squares[1]
    row = lax.broadcasted_iota(jnp.int32, (16, 128), 0)
    col = lax.broadcasted_iota(jnp.int32, (16, 128), 1)
    per_row = jnp.sum(both, axis=1, keepdims=True)
    sq0 = jnp.sum(per_row[0:8], axis=0, keepdims=True)
    sq1 = jnp.sum(per_row[8:16], axis=0, keepdims=True)
    square = jnp.where(row < 8, sq0, sq1)
    square_hi = square.astype(BF).astype(F32)
    square = jnp.where(col < 64, square_hi, square - square_hi)

    def pack_rows(index):
        return pl.ds(pl.multiple_of(index * 16, 16), 16)

    third = []
    for s in range(2):
        value = sums[s] * gpk[s]
        if s == 0:
            value = jnp.where(row % 8 == 7, square, value)
        region = recv3.at[s, pack_rows(there[s])]
        recv3[s, pack_rows(there[s]), :] = value.astype(BF)
        for k in range(1, 8):
            copy = remote(region, region, p3_ss.at[s, k], p3_rs.at[s, k], along(s, False, k))
            copy.start()
            third.append(copy)
    for copy in pending:
        copy.wait_send()

    normed = (n0, n1)

    def n_rows(core, index):
        return pl.ds(pl.multiple_of((core * 8 + index) * 16, 16), 16)

    fourth = []
    for s in range(2):
        for k in range(1, 8):
            landed(
                recv3.at[s, pack_rows((there[s] - k + 8) % 8)], p3_ss.at[s, k], p3_rs.at[s, k]
            )
        unp[s] = recv3[s].astype(F32)
        count = PAIRS + 1 - s
        rows = [
            jnp.concatenate(
                [unp[s, pl.ds(p * 8 + k, 8, stride=16), :] for k in range(count)], axis=1
            )
            for p in range(2)
        ]
        normed[s][n_rows(c, here[s]), :] = jnp.concatenate(rows, axis=0).astype(BF)
        region = normed[s].at[n_rows(c, here[s])]
        for k in range(1, 8):
            copy = remote(region, region, p4_ss.at[s, k], p4_rs.at[s, k], along(s, True, k))
            copy.start()
            fourth.append(copy)
        copy = remote(region, region, p5_ss.at[s, 0], p5_rs.at[s, 0], sibling)
        copy.start()
        fourth.append(copy)
    for copy in third:
        copy.wait_send()
    for k in range(1, 8):
        for s in range(2):
            region = normed[s].at[n_rows(c, (here[s] - k + 8) % 8)]
            landed(region, p4_ss.at[s, k], p4_rs.at[s, k])
            copy = remote(region, region, p5_ss.at[s, k], p5_rs.at[s, k], sibling)
            copy.start()
            fourth.append(copy)
    for k in range(8):
        for s in range(2):
            landed(
                normed[s].at[n_rows(sib, (here[s] - k + 8) % 8)], p5_ss.at[s, k], p5_rs.at[s, k]
            )

    part = dot(n0[:, 0:HALF], wc[0:HALF, :])
    part = part + swap_rows(dot(n1[...], wc[HALF : 2 * HALF, :]), perm)
    at = lax.broadcasted_iota(jnp.int32, (256, 128), 1)
    extra = part[:, 256:384]
    extra = jnp.where(at == 32, n0[:, HALF : HALF + 1].astype(F32), extra)
    extra = jnp.where(at == 33, n0[:, HALF + 64 : HALF + 65].astype(F32), extra)
    gs[:, 0:256] = part[:, 0:256].astype(BF)
    gs[:, 256:384] = extra.astype(BF)

    def quarter(index):
        return pl.ds(pl.multiple_of(index * 64, 64), 64)

    gx = []
    for k in range(1, 4):
        to = (t + k) % 4
        copy = remote(
            gs.at[quarter(to)], recvx.at[k], gx_ss.at[k], gx_rs.at[k], dev(Y, zc, to)
        )
        copy.start()
        gx.append(copy)
    for copy in fourth:
        copy.wait_send()
    value = gs[quarter(t), :].astype(F32)
    for k in range(1, 4):
        gx[k - 1].wait_recv()
        value = value + recvx[k].astype(F32)
    tail = value[:, 256:384]
    factor = lax.rsqrt((tail[:, 32:33] + tail[:, 33:34]) / D + EPS)
    up_tail = pltpu.roll(tail, 112, 1)

    def gated(gate, up):
        gate = gate * factor
        return gate / (1.0 + jnp.exp(-gate)) * (up * factor)

    column = lax.broadcasted_iota(jnp.int32, (64, 128), 1)
    hid[quarter(t), 0:128] = gated(value[:, 0:128], value[:, 128:256]).astype(BF)
    hid[quarter(t), 128:256] = jnp.where(
        column < 16, gated(jnp.where(column < 16, tail, 0.0), up_tail), 0.0
    ).astype(BF)
    hx = []
    region = hid.at[quarter(t)]
    for k in range(1, 4):
        copy = remote(region, region, hx_ss.at[k], hx_rs.at[k], dev(Y, zc, (t + k) % 4))
        copy.start()
        hx.append(copy)
    for copy in gx:
        copy.wait_send()
    for k in range(1, 4):
        landed(hid.at[quarter((t - k + 4) % 4)], hx_ss.at[k], hx_rs.at[k])
    a2[...] = swap_rows(hid[...].astype(F32), perm).astype(BF)
    for copy in hx:
        copy.wait_send()

    projected, pending = reduced(1, (hid, a2), wd)
    for s in range(2):
        value = rsd[s] + projected[s]
        for p in range(2):
            for k in range(PAIRS):
                n = s * PAIRS + k
                flat_row = value[p * 8 + k : p * 8 + k + 1, :]
                out_ref[0, p : p + 1, n * 128 : (n + 1) * 128] = flat_row.astype(BF)
    for copy in pending:
        copy.wait_send()
    hand.wait_send()


def body(
    cache, sent, slot_of, table, lengths, new_kv, queries, resid, gain, w_ov, w_gate, w_up, w_down
):
    smem = pl.BlockSpec(memory_space=pltpu.SMEM)
    vmem = pl.BlockSpec(memory_space=pltpu.VMEM)
    hbm = pl.BlockSpec(memory_space=pl.ANY)
    dma = pltpu.SemaphoreType.DMA
    scratch = [
        pltpu.VMEM((24, 64, 576), BF),
        pltpu.VMEM((4, 64, 576), BF),
        pltpu.VMEM((128, 576), BF),
        pltpu.VMEM((2, 64, 576), BF),
        pltpu.VMEM((256, 1792), BF),
        pltpu.VMEM((1792, 144), BF),
        pltpu.VMEM((1792, 144), BF),
        pltpu.VMEM((1792, 384), BF),
        pltpu.VMEM((256, 1792), BF),
        pltpu.VMEM((4, 2, 16, 640), BF),
        pltpu.VMEM((4, 2, 16, 640), BF),
        pltpu.VMEM((2, 16, 512), BF),
        pltpu.VMEM((8, 16, 512), BF),
        pltpu.VMEM((4, 128, 128), F32),
        pltpu.VMEM((2, 128, 256), BF),
        pltpu.VMEM((256, 256), BF),
        pltpu.VMEM((256, 256), BF),
        pltpu.VMEM((3, 256, 128), F32),
        pltpu.VMEM((2, 2, 128, HALF), BF),
        pltpu.VMEM((2, 2, 128, HALF), BF),
        pltpu.VMEM((2, 128, HALF), F32),
        pltpu.VMEM((2, 2, 128, HALF), BF),
        pltpu.VMEM((2, 2, 8, 16, HALF), BF),
        pltpu.VMEM((2, 128, 128), F32),
        pltpu.VMEM((2, 2, 128, 128), BF),
        pltpu.VMEM((2, 2, 8, 16, 128), BF),
        pltpu.VMEM((2, 16, 128), F32),
        pltpu.VMEM((2, 16, 128), F32),
        pltpu.VMEM((2, 128, 128), BF),
        pltpu.VMEM((2, 128, 128), F32),
        pltpu.VMEM((256, HALF + 128), BF),
        pltpu.VMEM((256, HALF), BF),
        pltpu.VMEM((256, 384), BF),
        pltpu.VMEM((4, 64, 384), BF),
        pltpu.VMEM((256, 256), BF),
        pltpu.VMEM((5, 128, 128), F32),
        dma((6,)),
        dma((2,)),
        dma((4,)),
        dma((4,)),
        dma((2,)),
        dma((2,)),
        dma((4,)),
        dma((4,)),
        dma((16,)),
        dma((16,)),
        dma((2, 2)),
        dma((2, 2)),
        dma((2, 2, 8)),
        dma((2, 2, 8)),
        dma((2, 2, 8)),
        dma((2, 2, 8)),
        dma((2, 8)),
        dma((2, 8)),
        dma((2, 8)),
        dma((2, 8)),
        dma((2, 8)),
        dma((2, 8)),
        dma((4,)),
        dma((4,)),
        dma((4,)),
        dma((4,)),
    ]
    return pl.pallas_call(
        kernel,
        out_shape=jax.ShapeDtypeStruct((1, 2, 1792), BF),
        in_specs=[smem, smem, smem, vmem, vmem, vmem] + [hbm] * 7,
        out_specs=vmem,
        scratch_shapes=scratch,
        compiler_params=pltpu.CompilerParams(
            collective_id=0, has_side_effects=True, vmem_limit_bytes=48 * 1024 * 1024
        ),
        cost_estimate=pl.CostEstimate(
            flops=2_000_000_000, bytes_accessed=6_000_000, transcendentals=250_000
        ),
    )(
        lengths,
        table,
        slot_of,
        new_kv,
        resid,
        gain.reshape(1, 1792),
        cache,
        sent,
        queries,
        w_ov,
        w_gate,
        w_up,
        w_down,
    )


def solution(mesh):
    in_specs = (
        P(("section", "dp"), "tp", None, None),
        P(("section", "dp"), "tp", None, None),
        P(("section", "dp"), "tp"),
        P(("section", "dp"), "tp"),
        P(("section", "dp")),
        P(("section", "dp"), None, None),
        P(("section", "dp"), None, None, None),
        P(("section", "dp"), None, "tp"),
        P("tp"),
        P(("section", "dp"), "tp"),
        P("tp", ("section", "dp")),
        P("tp", ("section", "dp")),
        P(("section", "dp"), "tp"),
    )
    out_specs = P(("section", "dp"), None, "tp")
    return jax.shard_map(body, mesh=mesh, in_specs=in_specs, out_specs=out_specs, check_vma=False)
```

time: 855 us -> 117 us (0.14)
  waiting for transfers between devices: 485 us -> 0 us
  other arithmetic: 190 us -> 0 us
  Pallas kernels: 0 us -> 109 us
  local copies, waits for them, and re-layouts: 113 us -> 6.52 us
  starting transfers between devices: 23.9 us -> 0 us
  blocking collectives: 21 us -> 0 us
  between operations: 14.1 us -> 0.88 us
    psum x2 -> x0, waiting for transfers between devices: 239 us -> none  [the longest x1 191 us: body(): resid_sum = lax.psum(partial_value, ('section', 'dp'))]
    unnamed x5 -> x0, waiting for transfers between devices: 201 us -> none
    unnamed x1 -> x0, other arithmetic: 179 us -> none
    pallas_call x0 -> x1, Pallas kernels: none -> 109 us  [body(): pl.pallas_call(kernel, out_shape=jax.ShapeDtypeStruct((1, 2, 1792), BF),...]
    unnamed x29 -> x21, local copies, waits for them, and re-layouts: 50.3 us -> 5.82 us
    all_to_all x1 -> x0, local copies, waits for them, and re-layouts: 30.6 us -> none  [body(): lax.all_to_all(flat, ('section', 'dp'), split_axis=2, concat_axis=0, tile...]
    reshape x4 -> x1, local copies, waits for them, and re-layouts: 26 us -> 0.7 us  [body(): gain.reshape(1, 1792)]
    all_gather x1 -> x0, waiting for transfers between devices: 24.4 us -> none  [joined(): everything = jax.tree.map(lambda part: lax.all_gather(part, axis), x)]
  transfers between devices with their start and end apart: 6 -> 0, of which waited for: 6 -> 0; matrix products, arithmetic and copies ran while one was open for 0% -> 0% of each run, Pallas kernels for 0% -> 0%
where the time goes in v1:
time: 117 us
  Pallas kernels  109 us (93%)
  local copies, waits for them, and re-layouts  6.52 us (6%)
    pallas_call x1, Pallas kernels, body(): pl.pallas_call(kernel, out_shape=jax.ShapeDtypeStruct((1, 2, 1792), BF),...  109 us
    unnamed x21, local copies, waits for them, and re-layouts  5.82 us

profile of v1, /device:TPU:1, one launch (start us, length us, event | category | flops | bytes accessed | tf_op | source)
XLA Modules:
  0.0 116.6 jit_solution(11871042779959896784)
XLA Ops:
  0.0 0.0 copy-start.2
  0.0 0.0 copy-start.1
  0.0 0.0 copy-start.5
  0.0 0.0 copy-start.4
  0.0 0.0 copy-start.6
  0.0 0.0 copy-start.7
  0.0 0.0 copy-start.8
  0.8 0.7 reshape.3.gain_ref
  1.5 1.3 %copy.14.wgate_ref = bf16[1792,144]{1,0:T(8,128)(2,1)S(1)} copy(bf16[1792,144]{0,1:T(8,128)(2,1)} %param.23) | data formatting | bytes 1032192 | tf_op args[10]
  2.9 1.3 %copy.15.wup_ref = bf16[1792,144]{1,0:T(8,128)(2,1)S(1)} copy(bf16[1792,144]{0,1:T(8,128)(2,1)} %param.24) | data formatting | bytes 1032192 | tf_op args[11]
  4.2 0.0 copy-done.2
  4.2 0.0 copy-done.1
  4.2 0.0 copy-done.5
  4.2 0.0 copy-done.4
  4.2 0.0 copy-done.6
  4.3 0.0 copy-done.7
  4.3 0.0 copy-done.8
  4.3 0.0 copy-start
  4.3 1.5 %copy-done = bf16[1,24,64,576]{3,2,1,0:T(8,128)(2,1)S(1)} copy-done((bf16[1,24,64,576]{3,2,1,0:T(8,128)(2,1)S(1)}, bf16[1,24,64,576]{3,2,1,0:T(8,128)(2,1)}, u32[]{:S(2)}) %copy-start) | copy-done | bytes 1769496
  5.8 0.0 copy-start.3
  5.8 1.0 copy-done.3
  6.8 109.2 %shard_map.127 = bf16[1,2,1792]{2,1,0:T(2,128)(2,1)S(1)} custom-call(s32[1]{0:T(128)S(6)} %copy.17.lengths_ref, s32[1,24]{1,0:T(1,128)S(1)} %copy-done.7, s32[1,4]{1,0:T(1,128)S(1)} %copy-done.8, bf16[1,2,576]{2,1,0:T(2,128)(2,1)S(1)} %copy-done.6, bf16[1,2,1792]{2,1,0:T(2,128)(2,1)S(1)} %copy-done.5, f32[1,1792]{1,0:T(1,128)S(1)} %reshape.3.gain_ref, ...), custom_call_target="tpu_custom_call" | custom-call | flops 2000000000 | bytes 6000000 | tf_op jit(solution)/shard_map/pallas_call | solution.py:658
  116.0 0.6 copy.18
Async XLA Ops:
  0.0 4.2 %copy-start.2 = (bf16[144,1792]{1,0:T(8,128)(2,1)S(1)}, bf16[144,1792]{1,0:T(8,128)(2,1)}, u32[]{:S(2)}) copy-start(bf16[144,1792]{1,0:T(8,128)(2,1)} %wdown_ref.1) | copy-start | bytes 1548292
  0.0 4.2 %copy-start.1 = (bf16[256,1792]{1,0:T(8,128)(2,1)S(1)}, bf16[256,1792]{1,0:T(8,128)(2,1)}, u32[]{:S(2)}) copy-start(bf16[256,1792]{1,0:T(8,128)(2,1)} %wov_ref.1) | copy-start | bytes 2752516
  0.0 4.2 %copy-start.5 = (bf16[1,2,1792]{2,1,0:T(2,128)(2,1)S(1)}, bf16[1,2,1792]{2,1,0:T(2,128)(2,1)}, u32[]{:S(2)}) copy-start(bf16[1,2,1792]{2,1,0:T(2,128)(2,1)} %resid_ref.1) | copy-start | bytes 21508
  0.0 4.2 %copy-start.4 = (bf16[1,2,64,576]{3,2,1,0:T(8,128)(2,1)S(1)}, bf16[1,2,64,576]{3,2,1,0:T(8,128)(2,1)}, u32[]{:S(2)}) copy-start(bf16[1,2,64,576]{3,2,1,0:T(8,128)(2,1)} %query_ref.1) | copy-start | bytes 442372
  0.0 4.2 %copy-start.6 = (bf16[1,2,576]{2,1,0:T(2,128)(2,1)S(1)}, bf16[1,2,576]{2,1,0:T(2,128)(2,1)}, u32[]{:S(2)}) copy-start(bf16[1,2,576]{2,1,0:T(2,128)(2,1)} %new_ref.1) | copy-start | bytes 6916
  0.0 4.2 %copy-start.7 = (s32[1,24]{1,0:T(1,128)S(1)}, s32[1,24]{1,0:T(1,128)}, u32[]{:S(2)}) copy-start(s32[1,24]{1,0:T(1,128)} %table_ref.1) | copy-start | bytes 292
  0.0 4.2 %copy-start.8 = (s32[1,4]{1,0:T(1,128)S(1)}, s32[1,4]{1,0:T(1,128)}, u32[]{:S(2)}) copy-start(s32[1,4]{1,0:T(1,128)} %slot_ref.1) | copy-start | bytes 52
  4.3 1.5 %copy-start = (bf16[1,24,64,576]{3,2,1,0:T(8,128)(2,1)S(1)}, bf16[1,24,64,576]{3,2,1,0:T(8,128)(2,1)}, u32[]{:S(2)}) copy-start(bf16[1,24,64,576]{3,2,1,0:T(8,128)(2,1)} %cache_ref.1) | copy-start | bytes 5308420
  5.8 1.0 copy-start.3

commit v2 on v1

v2 whole, which is shorter than its diff:
```python
import functools

import jax
import jax.numpy as jnp
from jax import lax
from jax.experimental import pallas as pl
from jax.experimental.pallas import tpu as pltpu
from jax.sharding import PartitionSpec as P

D = 7168
LAT = 512
SCALE = 192.0 ** (-0.5)
EPS = 1e-06
LOW = -1e30
FLOOR = -1e20
MESH = pl.DeviceIdType.MESH
BF = jnp.bfloat16
F32 = jnp.float32
HALF = 896
PAIRS = 7

NT = (((1,), (1,)), ((), ()))


def dot(a, b):
    return jnp.dot(a, b, preferred_element_type=F32)


def dot_nt(a, b):
    return lax.dot_general(a, b, NT, preferred_element_type=F32)


def swap_rows(x, scratch):
    blocks = x.shape[1] // 128
    for c in range(2):
        for a in range(8):
            for p in range(2):
                row = c * 128 + a * 16 + p * 8
                for n in range(blocks):
                    scratch[n, pl.ds(c * 128 + p * 8 + a, 8, stride=16), :] = x[
                        row : row + 8, n * 128 : (n + 1) * 128
                    ]
    return jnp.concatenate([scratch[n] for n in range(blocks)], axis=1)


def kernel(
    lengths_ref,
    table_ref,
    slot_ref,
    new_ref,
    resid_ref,
    gain_ref,
    cache_ref,
    sent_ref,
    query_ref,
    wov_ref,
    wgate_ref,
    wup_ref,
    wdown_ref,
    out_ref,
    kv,
    kx,
    kn,
    qs,
    qx,
    qf,
    wov,
    wc,
    wd,
    l1s,
    l1r,
    zb,
    zr,
    lx,
    un,
    af,
    a1,
    a2,
    perm,
    core_send,
    core_recv,
    tot,
    send1,
    recv1,
    pack,
    send2,
    recv2,
    rsd,
    gpk,
    recv3,
    unp,
    n0,
    n1,
    gs,
    recvx,
    hid,
    flat,
    count,
    load_sem,
    q_ss,
    q_rs,
    l1_ss,
    l1_rs,
    lx_ss,
    lx_rs,
    lz_ss,
    lz_rs,
    core_ss,
    core_rs,
    p1_ss,
    p1_rs,
    p2_ss,
    p2_rs,
    p3_ss,
    p3_rs,
    p4_ss,
    p4_rs,
    p5_ss,
    p5_rs,
    gx_ss,
    gx_rs,
    hx_ss,
    hx_rs,
):
    dp = lax.axis_index("dp")
    t = lax.axis_index("tp")
    Y = lax.axis_index("section") * 4 + dp // 16
    zc = dp % 16
    z = zc // 2
    c = zc % 2
    sib = 1 - c

    def dev(y_, zc_, t_):
        return (y_ // 4, (y_ % 4) * 16 + zc_, t_)

    def along(s, first, k):
        if (s == 0) == first:
            return dev(Y, ((z + k) % 8) * 2 + c, t)
        return dev((Y + k) % 8, zc, t)

    here = (z, Y)
    there = (Y, z)
    sibling = dev(Y, z * 2 + sib, t)

    def remote(src, dst, ss, rs, to):
        return pltpu.make_async_remote_copy(
            src_ref=src, dst_ref=dst, send_sem=ss, recv_sem=rs, device_id=to, device_id_type=MESH
        )

    opened = []

    def send(src, dst, ss, rs, to):
        copy = remote(src, dst, ss, rs, to)
        copy.start()
        opened.append(copy)
        return copy

    def drain(count):
        for copy in opened[:count]:
            copy.wait_send()
        del opened[:count]

    def landed(region, ss, rs):
        remote(region, region, ss, rs, sibling).wait_recv()

    loads = [
        pltpu.make_async_copy(cache_ref.at[0], kv, load_sem.at[0]),
        pltpu.make_async_copy(query_ref.at[0], qs, load_sem.at[1]),
        pltpu.make_async_copy(wov_ref, wov, load_sem.at[2]),
        pltpu.make_async_copy(wgate_ref, wc.at[pl.ds(0, 144)], load_sem.at[3]),
        pltpu.make_async_copy(wup_ref, wc.at[pl.ds(144, 144)], load_sem.at[4]),
        pltpu.make_async_copy(wdown_ref, wd.at[pl.ds(0, 144)], load_sem.at[5]),
        pltpu.make_async_copy(sent_ref.at[0], kx, load_sem.at[6]),
        pltpu.make_async_copy(lengths_ref, count, load_sem.at[7]),
    ]
    for load in loads:
        load.start()

    waiting = dict(enumerate(loads))

    def loaded(n):
        waiting.pop(n).wait()

    def finish():
        drain(len(opened))
        for load in waiting.values():
            load.wait()
        out_ref[...] = jnp.zeros((1, 2, 1792), BF)

    barrier = pltpu.get_barrier_semaphore()
    for k in range(1, 8):
        pl.semaphore_signal(barrier, inc=1, device_id=dev((Y + k) % 8, zc, t), device_id_type=MESH)
    for k in range(1, 16):
        pl.semaphore_signal(barrier, inc=1, device_id=dev(Y, (zc + k) % 16, t), device_id_type=MESH)
    for k in range(1, 4):
        pl.semaphore_signal(barrier, inc=1, device_id=dev(Y, zc, (t + k) % 4), device_id_type=MESH)
    for j in range(2):
        for i in range(4):

            def greet():
                to = dev((Y + 16 - t - 4 * j) % 8, zc, i)
                pl.semaphore_signal(barrier, inc=1, device_id=to, device_id_type=MESH)

            if i == 0 and j == 0:
                pl.when(t != 0)(greet)
            else:
                greet()
    pl.semaphore_wait(barrier, jnp.where(t == 0, 32, 33))

    lane = lax.broadcasted_iota(jnp.int32, (1, 128), 1)
    loaded(7)
    length = count[0]
    late = [length - table_ref[0, slot_ref[0, e]] * 64 for e in range(4)]
    within = jnp.zeros((1, 128), jnp.int32)
    for e in range(4):
        within = jnp.where(lane == e, late[e], within)
    within = jnp.clip(within, 0, 64).astype(F32)
    loaded(1)
    q = qs[...].reshape(128, 576)
    qx[:, 0:512] = q[:, 0:512]
    qx[:, 512:640] = jnp.concatenate(
        [q[:, 512:576].astype(F32), jnp.broadcast_to(within[:, 0:64], (128, 64))], axis=1
    ).astype(BF)

    def q_rows(index):
        return pl.ds(pl.multiple_of(index * 32, 32), 32)

    first_q = send(
        qx.at[q_rows(t)], qf.at[q_rows(t)], q_ss.at[0], q_rs.at[0], dev((Y + 4) % 8, zc, t)
    )

    resid = resid_ref[0].astype(F32)
    for s in range(2):
        rsd[s] = jnp.zeros((16, 128), F32)
        gpk[s] = jnp.zeros((16, 128), F32)
        for p in range(2):
            for k in range(PAIRS):
                n = s * PAIRS + k
                rsd[s, p * 8 + k : p * 8 + k + 1, :] = resid[p : p + 1, n * 128 : (n + 1) * 128]
                gpk[s, p * 8 + k : p * 8 + k + 1, :] = gain_ref[n : n + 1, :]
    wd[pl.ds(144, 112)] = jnp.zeros((112, 1792), BF)
    kn[...] = jnp.zeros((128, 576), BF)
    kn[0:2, :] = new_ref[0]

    inside = lane % 64

    def bias_of(first, second):
        return jnp.where(inside < jnp.where(lane < 64, first, second), 0.0, LOW)

    limits = []
    for slot in range(24):
        limit = length - table_ref[0, slot] * 64
        for e in range(4):
            limit = jnp.where(slot_ref[0, e] == slot, 0, limit)
        limits.append(limit)
    bias = jnp.concatenate([bias_of(limits[i], limits[i + 1]) for i in range(0, 24, 2)], axis=1)
    head = lax.broadcasted_iota(jnp.int32, (128, 128), 0)
    entry = lax.broadcasted_iota(jnp.int32, (128, 128), 1)
    fresh = jnp.where(t == 0, 1, 0)
    bias_n = jnp.where(entry < jnp.where(head < 64, 1, 2) * fresh, 0.0, LOW)

    def partial(kind, q, chunks):
        scores = [dot_nt(q, keys) * SCALE + bias for keys, bias in chunks]
        top = functools.reduce(
            jnp.maximum, [jnp.max(score, axis=1, keepdims=True) for score in scores]
        )
        top = jnp.maximum(top, FLOOR)
        weights = [jnp.exp(score - top) for score in scores]
        total = functools.reduce(jnp.add, [jnp.sum(w, axis=1, keepdims=True) for w in weights])
        acc = functools.reduce(
            jnp.add, [dot(w.astype(BF), keys[:, :LAT]) for w, (keys, _) in zip(weights, chunks)]
        )
        total = jnp.where(total > 0.0, total, 1.0)
        acc = acc / total
        lse = top + jnp.log(total)
        hi = lse.astype(BF).astype(F32)
        mid = (lse - hi).astype(BF).astype(F32)
        low = lse - hi - mid
        for n in range(4):
            flat[kind, n] = acc[:, n * 128 : (n + 1) * 128]
        flat[kind, 4] = jnp.where(entry < 32, hi, jnp.where(entry < 64, mid, low))

    def spread(kind):
        for k in range(8):
            block = (Y + k) % 8
            rows = []
            for p in range(2):
                at = pl.ds(pl.multiple_of(p * 64 + block * 8, 8), 8)
                rows.append(jnp.concatenate([flat[kind, n, at, :] for n in range(5)], axis=1))
            l1s[kind, k] = jnp.concatenate(rows, axis=0).astype(BF)
            if k:
                send(
                    l1s.at[kind, k],
                    l1r.at[kind, k // 4, t],
                    l1_ss.at[kind, k],
                    l1_rs.at[kind, k // 4, t],
                    dev(block, zc, k % 4),
                )

        @pl.when(t == 0)
        def _():
            l1r[kind, 0, 0] = l1s[kind, 0]

        @pl.when(t != 0)
        def _():
            to_zero(kind).start()

    def to_zero(kind):
        return remote(
            l1s.at[kind, 0],
            l1r.at[kind, 0, t],
            l1_ss.at[kind, 0],
            l1_rs.at[kind, 0, t],
            dev(Y, zc, 0),
        )

    loaded(0)
    partial(0, q, [(kv[...].reshape(1536, 576), bias), (kn[...], bias_n)])

    landed(qf.at[q_rows(t)], q_ss.at[0], q_rs.at[0])
    region = qf.at[q_rows(t)]
    for k in range(1, 4):
        send(region, region, q_ss.at[k], q_rs.at[k], dev(Y, zc, (t + k) % 4))
    spread(0)
    drain(1)
    bounds = qf[q_rows(t), 512:640].astype(F32)[0:1, :]
    spot = inside.astype(F32)
    bias_x = jnp.concatenate(
        [
            jnp.where(
                spot < jnp.where(lane < 64, bounds[:, 64 + e : 65 + e], bounds[:, 65 + e : 66 + e]),
                0.0,
                LOW,
            )
            for e in (0, 2)
        ],
        axis=1,
    )
    loaded(6)
    for k in range(1, 4):
        landed(qf.at[q_rows((t - k + 4) % 4)], q_ss.at[k], q_rs.at[k])
    partial(1, qf[:, 0:576], [(kx[...].reshape(256, 576), bias_x)])
    spread(1)
    drain(3 + 7)

    def arrived(kind, j, i):
        def wait():
            landed(l1r.at[kind, j, i], l1_ss.at[kind, 0], l1_rs.at[kind, j, i])

        if i == 0 and j == 0:
            pl.when(t != 0)(wait)
        else:
            wait()

    for kind in range(2):
        for j in range(2):
            for i in range(4):
                arrived(kind, j, i)
    for j in range(2):
        parts = [
            l1r[kind, j ^ kind, i].astype(F32) for kind in range(2) for i in range(4)
        ]
        lses = [part[:, 512:513] + part[:, 544:545] + part[:, 576:577] for part in parts]
        best = functools.reduce(jnp.maximum, lses)
        shares = [jnp.exp(value - best) for value in lses]
        norm = functools.reduce(jnp.add, shares)
        mixed = functools.reduce(
            jnp.add, [part[:, :LAT] * share for part, share in zip(parts, shares)]
        )
        mixed = mixed / norm
        for p in range(2):
            for n in range(4):
                zb[n // 2, pl.ds(j * 4 + p * 2 + n % 2, 8, stride=8), :] = mixed[
                    p * 8 : p * 8 + 8, n * 128 : (n + 1) * 128
                ]

    def z_slot(zc_):
        return (zc_ % 2) * 8 + zc_ // 2

    for k in range(1, 16):
        to = (zc + k) % 16
        send(
            zb.at[to % 2, pl.ds(pl.multiple_of((to // 2) * 8, 8), 8)],
            zr.at[z_slot(zc)],
            lz_ss.at[k],
            lz_rs.at[k],
            dev(Y, to, t),
        )
    zr[z_slot(zc)] = zb[c, pl.ds(pl.multiple_of(z * 8, 8), 8), :]
    drain(7)

    @pl.when(t != 0)
    def _():
        to_zero(0).wait_send()
        to_zero(1).wait_send()

    loaded(2)
    loaded(3)
    loaded(4)
    loaded(5)
    for k in range(1, 16):
        landed(zr.at[z_slot((zc - k + 16) % 16)], lz_ss.at[k], lz_rs.at[k])
    lx[t] = zr[...].reshape(128, 128).astype(BF)
    for k in range(1, 4):
        send(lx.at[t], lx.at[t], lx_ss.at[k], lx_rs.at[k], dev(Y, zc, (t + k) % 4))
    drain(15)
    for k in range(4):
        source = (t - k + 4) % 4
        if k:
            landed(lx.at[source], lx_ss.at[k], lx_rs.at[k])
        un[k] = lx[source].astype(F32)
        for j in range(2):
            y_from = (Y - source - 4 * j + 8) % 8
            for p in range(2):
                for n in range(2):
                    for core in range(2):
                        rows = un[k, pl.ds(core * 64 + j * 4 + p * 2 + n, 8, stride=8), :]
                        af[0, n, pl.ds(core * 128 + p * 8 + y_from, 8, stride=16), :] = rows
                        at = pl.multiple_of(core * 128 + y_from * 16 + p * 8, 8)
                        af[1, n, pl.ds(at, 8), :] = rows
    a1[...] = jnp.concatenate([af[0, 0], af[0, 1]], axis=1).astype(BF)
    a2[...] = jnp.concatenate([af[1, 0], af[1, 1]], axis=1).astype(BF)
    drain(3)
    def reduced(u, operands, weight):
        before = len(opened)
        started = []
        for s in range(2):
            columns = slice(s * HALF, (s + 1) * HALF)
            rows = pl.ds(pl.multiple_of(sib * 128, 128), 128)
            core_send[u, s] = dot(operands[s][rows, :], weight[:, columns]).astype(BF)
            copy = send(
                core_send.at[u, s],
                core_recv.at[u, s],
                core_ss.at[u, s],
                core_rs.at[u, s],
                sibling,
            )
            started.append(copy)
        for s in range(2):
            columns = slice(s * HALF, (s + 1) * HALF)
            rows = pl.ds(pl.multiple_of(c * 128, 128), 128)
            tot[s] = dot(operands[s][rows, :], weight[:, columns])
        first = []
        for s in range(2):
            started[s].wait_recv()
            tot[s] = tot[s] + core_recv[u, s].astype(F32)
            send1[u, s] = tot[s].astype(BF)
            copies = []
            for k in range(1, 8):
                block = (here[s] + k) % 8
                copy = send(
                    send1.at[u, s, pl.ds(pl.multiple_of(block * 16, 16), 16)],
                    recv1.at[u, s, k],
                    p1_ss.at[u, s, k],
                    p1_rs.at[u, s, k],
                    along(s, True, k),
                )
                copies.append(copy)
            first.append(copies)
        drain(before + 2)
        second = []
        for s in range(2):
            part = tot[s, pl.ds(pl.multiple_of(here[s] * 16, 16), 16), :]
            for k in range(1, 8):
                first[s][k - 1].wait_recv()
                part = part + recv1[u, s, k].astype(F32)
            for p in range(2):
                for k in range(PAIRS):
                    pack[s, pl.ds(p * 8 + k, 8, stride=16), :] = part[
                        p * 8 : p * 8 + 8, k * 128 : (k + 1) * 128
                    ]
                pack[s, pl.ds(p * 8 + PAIRS, 8, stride=16), :] = jnp.zeros((8, 128), F32)
            send2[u, s] = pack[s].astype(BF)
            copies = []
            for k in range(1, 8):
                block = (there[s] + k) % 8
                copy = send(
                    send2.at[u, s, pl.ds(pl.multiple_of(block * 16, 16), 16)],
                    recv2.at[u, s, k],
                    p2_ss.at[u, s, k],
                    p2_rs.at[u, s, k],
                    along(s, False, k),
                )
                copies.append(copy)
            second.append(copies)
        drain(14)
        result = []
        for s in range(2):
            part = pack[s, pl.ds(pl.multiple_of(there[s] * 16, 16), 16), :]
            for k in range(1, 8):
                second[s][k - 1].wait_recv()
                part = part + recv2[u, s, k].astype(F32)
            result.append(part)
        return result

    attended = reduced(0, (a1, a2), wov)

    sums = []
    squares = []
    for s in range(2):
        value = attended[s] + rsd[s]
        rsd[s] = value
        sums.append(value)
        squares.append(value * value)
    both = squares[0] + squares[1]
    row = lax.broadcasted_iota(jnp.int32, (16, 128), 0)
    col = lax.broadcasted_iota(jnp.int32, (16, 128), 1)
    per_row = jnp.sum(both, axis=1, keepdims=True)
    sq0 = jnp.sum(per_row[0:8], axis=0, keepdims=True)
    sq1 = jnp.sum(per_row[8:16], axis=0, keepdims=True)
    square = jnp.where(row < 8, sq0, sq1)
    square_hi = square.astype(BF).astype(F32)
    square = jnp.where(col < 64, square_hi, square - square_hi)

    def pack_rows(index):
        return pl.ds(pl.multiple_of(index * 16, 16), 16)

    for s in range(2):
        value = sums[s] * gpk[s]
        if s == 0:
            value = jnp.where(row % 8 == 7, square, value)
        region = recv3.at[s, pack_rows(there[s])]
        recv3[s, pack_rows(there[s]), :] = value.astype(BF)
        for k in range(1, 8):
            send(region, region, p3_ss.at[s, k], p3_rs.at[s, k], along(s, False, k))
    drain(14)

    normed = (n0, n1)

    def n_rows(core, index):
        return pl.ds(pl.multiple_of((core * 8 + index) * 16, 16), 16)

    for s in range(2):
        for k in range(1, 8):
            landed(
                recv3.at[s, pack_rows((there[s] - k + 8) % 8)], p3_ss.at[s, k], p3_rs.at[s, k]
            )
        unp[s] = recv3[s].astype(F32)
        count = PAIRS + 1 - s
        rows = [
            jnp.concatenate(
                [unp[s, pl.ds(p * 8 + k, 8, stride=16), :] for k in range(count)], axis=1
            )
            for p in range(2)
        ]
        normed[s][n_rows(c, here[s]), :] = jnp.concatenate(rows, axis=0).astype(BF)
        region = normed[s].at[n_rows(c, here[s])]
        for k in range(1, 8):
            send(region, region, p4_ss.at[s, k], p4_rs.at[s, k], along(s, True, k))
        send(region, region, p5_ss.at[s, 0], p5_rs.at[s, 0], sibling)
    drain(14)
    for k in range(1, 8):
        for s in range(2):
            region = normed[s].at[n_rows(c, (here[s] - k + 8) % 8)]
            landed(region, p4_ss.at[s, k], p4_rs.at[s, k])
            send(region, region, p5_ss.at[s, k], p5_rs.at[s, k], sibling)
    for k in range(8):
        for s in range(2):
            landed(
                normed[s].at[n_rows(sib, (here[s] - k + 8) % 8)], p5_ss.at[s, k], p5_rs.at[s, k]
            )

    part = dot_nt(n0[:, 0:HALF], wc[:, 0:HALF])
    other = dot_nt(n1[...], wc[:, HALF : 2 * HALF])
    nothing = jnp.zeros((256, 96), F32)
    part = jnp.concatenate([part, nothing], axis=1)
    part = part + swap_rows(jnp.concatenate([other, nothing], axis=1), perm)
    at = lax.broadcasted_iota(jnp.int32, (256, 128), 1)
    extra = part[:, 256:384]
    extra = jnp.where(at == 32, n0[:, HALF : HALF + 1].astype(F32), extra)
    extra = jnp.where(at == 33, n0[:, HALF + 64 : HALF + 65].astype(F32), extra)
    gs[:, 0:256] = part[:, 0:256].astype(BF)
    gs[:, 256:384] = extra.astype(BF)

    def quarter(index):
        return pl.ds(pl.multiple_of(index * 64, 64), 64)

    gx = []
    for k in range(1, 4):
        to = (t + k) % 4
        gx.append(send(gs.at[quarter(to)], recvx.at[k], gx_ss.at[k], gx_rs.at[k], dev(Y, zc, to)))
    drain(30)
    value = gs[quarter(t), :].astype(F32)
    for k in range(1, 4):
        gx[k - 1].wait_recv()
        value = value + recvx[k].astype(F32)
    tail = value[:, 256:384]
    factor = lax.rsqrt((tail[:, 32:33] + tail[:, 33:34]) / D + EPS)
    ups = pltpu.roll(value, 240, 1)

    def gated(gate, up):
        gate = gate * factor
        return gate / (1.0 + jnp.exp(-gate)) * (up * factor)

    column = lax.broadcasted_iota(jnp.int32, (64, 256), 1)
    hid[quarter(t), :] = jnp.where(column < 144, gated(value[:, 0:256], ups[:, 0:256]), 0.0).astype(BF)
    region = hid.at[quarter(t)]
    for k in range(1, 4):
        send(region, region, hx_ss.at[k], hx_rs.at[k], dev(Y, zc, (t + k) % 4))
    drain(3)
    for k in range(1, 4):
        landed(hid.at[quarter((t - k + 4) % 4)], hx_ss.at[k], hx_rs.at[k])
    a2[...] = swap_rows(hid[...].astype(F32), perm).astype(BF)
    drain(3)

    projected = reduced(1, (hid, a2), wd)
    for s in range(2):
        value = rsd[s] + projected[s]
        for p in range(2):
            for k in range(PAIRS):
                n = s * PAIRS + k
                flat_row = value[p * 8 + k : p * 8 + k + 1, :]
                out_ref[0, p : p + 1, n * 128 : (n + 1) * 128] = flat_row.astype(BF)
    drain(len(opened))


def body(
    cache, sent, slot_of, table, lengths, new_kv, queries, resid, gain, w_ov, w_gate, w_up, w_down
):
    smem = pl.BlockSpec(memory_space=pltpu.SMEM)
    vmem = pl.BlockSpec(memory_space=pltpu.VMEM)
    hbm = pl.BlockSpec(memory_space=pl.ANY)
    dma = pltpu.SemaphoreType.DMA
    scratch = [
        pltpu.VMEM((24, 64, 576), BF),
        pltpu.VMEM((4, 64, 576), BF),
        pltpu.VMEM((128, 576), BF),
        pltpu.VMEM((2, 64, 576), BF),
        pltpu.VMEM((128, 640), BF),
        pltpu.VMEM((128, 640), BF),
        pltpu.VMEM((256, 1792), BF),
        pltpu.VMEM((288, 1792), BF),
        pltpu.VMEM((256, 1792), BF),
        pltpu.VMEM((2, 8, 16, 640), BF),
        pltpu.VMEM((2, 2, 4, 16, 640), BF),
        pltpu.VMEM((2, 64, 128), F32),
        pltpu.VMEM((16, 8, 128), F32),
        pltpu.VMEM((4, 128, 128), BF),
        pltpu.VMEM((4, 128, 128), F32),
        pltpu.VMEM((2, 2, 256, 128), F32),
        pltpu.VMEM((256, 256), BF),
        pltpu.VMEM((256, 256), BF),
        pltpu.VMEM((3, 256, 128), F32),
        pltpu.VMEM((2, 2, 128, HALF), BF),
        pltpu.VMEM((2, 2, 128, HALF), BF),
        pltpu.VMEM((2, 128, HALF), F32),
        pltpu.VMEM((2, 2, 128, HALF), BF),
        pltpu.VMEM((2, 2, 8, 16, HALF), BF),
        pltpu.VMEM((2, 128, 128), F32),
        pltpu.VMEM((2, 2, 128, 128), BF),
        pltpu.VMEM((2, 2, 8, 16, 128), BF),
        pltpu.VMEM((2, 16, 128), F32),
        pltpu.VMEM((2, 16, 128), F32),
        pltpu.VMEM((2, 128, 128), BF),
        pltpu.VMEM((2, 128, 128), F32),
        pltpu.VMEM((256, HALF + 128), BF),
        pltpu.VMEM((256, HALF), BF),
        pltpu.VMEM((256, 384), BF),
        pltpu.VMEM((4, 64, 384), BF),
        pltpu.VMEM((256, 256), BF),
        pltpu.VMEM((2, 5, 128, 128), F32),
        pltpu.SMEM((1,), jnp.int32),
        dma((8,)),
        dma((4,)),
        dma((4,)),
        dma((2, 8)),
        dma((2, 2, 4)),
        dma((4,)),
        dma((4,)),
        dma((16,)),
        dma((16,)),
        dma((2, 2)),
        dma((2, 2)),
        dma((2, 2, 8)),
        dma((2, 2, 8)),
        dma((2, 2, 8)),
        dma((2, 2, 8)),
        dma((2, 8)),
        dma((2, 8)),
        dma((2, 8)),
        dma((2, 8)),
        dma((2, 8)),
        dma((2, 8)),
        dma((4,)),
        dma((4,)),
        dma((4,)),
        dma((4,)),
    ]
    return pl.pallas_call(
        kernel,
        out_shape=jax.ShapeDtypeStruct((1, 2, 1792), BF),
        in_specs=[pl.BlockSpec(memory_space=pltpu.HBM), smem, smem, vmem, vmem, vmem] + [hbm] * 7,
        out_specs=vmem,
        scratch_shapes=scratch,
        compiler_params=pltpu.CompilerParams(
            collective_id=0, has_side_effects=True, vmem_limit_bytes=60 * 1024 * 1024
        ),
        cost_estimate=pl.CostEstimate(
            flops=2_000_000_000, bytes_accessed=6_000_000, transcendentals=250_000
        ),
    )(
        lengths,
        table,
        slot_of,
        new_kv,
        resid,
        gain.reshape(14, 128),
        cache,
        sent,
        queries,
        w_ov,
        w_gate.T,
        w_up.T,
        w_down,
    )


def solution(mesh):
    in_specs = (
        P(("section", "dp"), "tp", None, None),
        P(("section", "dp"), "tp", None, None),
        P(("section", "dp"), "tp"),
        P(("section", "dp"), "tp"),
        P(("section", "dp")),
        P(("section", "dp"), None, None),
        P(("section", "dp"), None, None, None),
        P(("section", "dp"), None, "tp"),
        P("tp"),
        P(("section", "dp"), "tp"),
        P("tp", ("section", "dp")),
        P("tp", ("section", "dp")),
        P(("section", "dp"), "tp"),
    )
    out_specs = P(("section", "dp"), None, "tp")
    return jax.shard_map(body, mesh=mesh, in_specs=in_specs, out_specs=out_specs, check_vma=False)
```

time: 117 us -> 102 us (0.87)
  Pallas kernels: 109 us -> 99.5 us
  local copies, waits for them, and re-layouts: 6.52 us -> 1.29 us
    pallas_call x1, Pallas kernels: 109 us -> 99.5 us  [body(): pl.pallas_call(kernel, out_shape=jax.ShapeDtypeStruct((1, 2, 1792), BF),...]
    unnamed x21 -> x1, local copies, waits for them, and re-layouts: 5.82 us -> 1.29 us
where the time goes in v2:
time: 102 us; the launch traced here: 101 us
  Pallas kernels  99.5 us (98%)
  local copies, waits for them, and re-layouts  1.29 us (1%)
    pallas_call x1, Pallas kernels, body(): pl.pallas_call(kernel, out_shape=jax.ShapeDtypeStruct((1, 2, 1792), BF),...  99.5 us

profile of v2, /device:TPU:1, one launch (start us, length us, event | category | flops | bytes accessed | tf_op | source)
XLA Modules:
  0.0 101.5 jit_solution(1269054079196768752)
XLA Ops:
  0.7 99.5 %shard_map.127 = bf16[1,2,1792]{2,1,0:T(2,128)(2,1)} custom-call(s32[1]{0:T(128)S(6)} %copy.15.lengths_ref, s32[1,24]{1,0:T(1,128)} %table_ref.1, s32[1,4]{1,0:T(1,128)} %slot_ref.1, bf16[1,2,576]{2,1,0:T(2,128)(2,1)} %new_ref.1, bf16[1,2,1792]{2,1,0:T(2,128)(2,1)} %resid_ref.1, f32[14,128]{1,0:T(8,128)} %bitcast.5, bf16[1,24,64,576]{3,2,1,0:T(8,128)(2,1)} %cache_ref.1, ...), custom_call_target="tpu_custom_call" | custom-call | flops 2000000000 | bytes 6000000 | tf_op jit(solution)/shard_map/pallas_call | solution.py:689
  100.2 1.3 %copy.16 = bf16[1,2,1792]{2,1,0:T(2,128)(2,1)} copy(bf16[1,2,1792]{2,1,0:T(2,128)(2,1)} %shard_map.127) | data formatting | bytes 14336

commit v3 on v2

--- a/solution.py
+++ b/solution.py
@@ -20,6 +20,7 @@
 PAIRS = 7
 
 NT = (((1,), (1,)), ((), ()))
+RING = (4, 3, 5, 2, 6, 1, 7)
 
 
 def dot(a, b):
@@ -30,17 +31,17 @@
     return lax.dot_general(a, b, NT, preferred_element_type=F32)
 
 
-def swap_rows(x, scratch):
+def swap_rows(x, scratch, core):
     blocks = x.shape[1] // 128
-    for c in range(2):
-        for a in range(8):
-            for p in range(2):
-                row = c * 128 + a * 16 + p * 8
-                for n in range(blocks):
-                    scratch[n, pl.ds(c * 128 + p * 8 + a, 8, stride=16), :] = x[
-                        row : row + 8, n * 128 : (n + 1) * 128
-                    ]
-    return jnp.concatenate([scratch[n] for n in range(blocks)], axis=1)
+    start = core * 128
+    for a in range(8):
+        for p in range(2):
+            row = a * 16 + p * 8
+            for n in range(blocks):
+                scratch[n, pl.ds(start + p * 8 + a, 8, stride=16), :] = x[
+                    row : row + 8, n * 128 : (n + 1) * 128
+                ]
+    return jnp.concatenate([scratch[n, start : start + 128, :] for n in range(blocks)], axis=1)
 
 
 def kernel(
@@ -70,7 +71,8 @@
     l1s,
     l1r,
     zb,
-    zr,
+    zs,
+    zt,
     lx,
     un,
     af,
@@ -95,7 +97,11 @@
     recvx,
     hid,
     flat,
-    count,
+    numbers,
+    slots,
+    newest,
+    base,
+    gains,
     load_sem,
     q_ss,
     q_rs,
@@ -171,7 +177,11 @@
         pltpu.make_async_copy(wup_ref, wc.at[pl.ds(144, 144)], load_sem.at[4]),
         pltpu.make_async_copy(wdown_ref, wd.at[pl.ds(0, 144)], load_sem.at[5]),
         pltpu.make_async_copy(sent_ref.at[0], kx, load_sem.at[6]),
-        pltpu.make_async_copy(lengths_ref, count, load_sem.at[7]),
+        pltpu.make_async_copy(table_ref, numbers, load_sem.at[7]),
+        pltpu.make_async_copy(slot_ref, slots, load_sem.at[8]),
+        pltpu.make_async_copy(new_ref, newest, load_sem.at[9]),
+        pltpu.make_async_copy(resid_ref, base, load_sem.at[10]),
+        pltpu.make_async_copy(gain_ref, gains, load_sem.at[11]),
     ]
     for load in loads:
         load.start()
@@ -188,10 +198,8 @@
         out_ref[...] = jnp.zeros((1, 2, 1792), BF)
 
     barrier = pltpu.get_barrier_semaphore()
-    for k in range(1, 8):
+    for k in RING:
         pl.semaphore_signal(barrier, inc=1, device_id=dev((Y + k) % 8, zc, t), device_id_type=MESH)
-    for k in range(1, 16):
-        pl.semaphore_signal(barrier, inc=1, device_id=dev(Y, (zc + k) % 16, t), device_id_type=MESH)
     for k in range(1, 4):
         pl.semaphore_signal(barrier, inc=1, device_id=dev(Y, zc, (t + k) % 4), device_id_type=MESH)
     for j in range(2):
@@ -205,12 +213,17 @@
                 pl.when(t != 0)(greet)
             else:
                 greet()
-    pl.semaphore_wait(barrier, jnp.where(t == 0, 32, 33))
+    for k in RING:
+        to = dev(Y, ((z + k) % 8) * 2 + c, t)
+        pl.semaphore_signal(barrier, inc=1, device_id=to, device_id_type=MESH)
+    pl.semaphore_signal(barrier, inc=1, device_id=sibling, device_id_type=MESH)
+    pl.semaphore_wait(barrier, jnp.where(t == 0, 25, 26))
 
     lane = lax.broadcasted_iota(jnp.int32, (1, 128), 1)
     loaded(7)
-    length = count[0]
-    late = [length - table_ref[0, slot_ref[0, e]] * 64 for e in range(4)]
+    loaded(8)
+    length = lengths_ref[0, 0]
+    late = [length - numbers[0, slots[0, e]] * 64 for e in range(4)]
     within = jnp.zeros((1, 128), jnp.int32)
     for e in range(4):
         within = jnp.where(lane == e, late[e], within)
@@ -229,7 +242,10 @@
         qx.at[q_rows(t)], qf.at[q_rows(t)], q_ss.at[0], q_rs.at[0], dev((Y + 4) % 8, zc, t)
     )
 
-    resid = resid_ref[0].astype(F32)
+    loaded(9)
+    loaded(10)
+    loaded(11)
+    resid = base[0].astype(F32)
     for s in range(2):
         rsd[s] = jnp.zeros((16, 128), F32)
         gpk[s] = jnp.zeros((16, 128), F32)
@@ -237,10 +253,10 @@
             for k in range(PAIRS):
                 n = s * PAIRS + k
                 rsd[s, p * 8 + k : p * 8 + k + 1, :] = resid[p : p + 1, n * 128 : (n + 1) * 128]
-                gpk[s, p * 8 + k : p * 8 + k + 1, :] = gain_ref[n : n + 1, :]
+                gpk[s, p * 8 + k : p * 8 + k + 1, :] = gains[n : n + 1, :]
     wd[pl.ds(144, 112)] = jnp.zeros((112, 1792), BF)
     kn[...] = jnp.zeros((128, 576), BF)
-    kn[0:2, :] = new_ref[0]
+    kn[0:2, :] = newest[0]
 
     inside = lane % 64
 
@@ -249,9 +265,9 @@
 
     limits = []
     for slot in range(24):
-        limit = length - table_ref[0, slot] * 64
+        limit = length - numbers[0, slot] * 64
         for e in range(4):
-            limit = jnp.where(slot_ref[0, e] == slot, 0, limit)
+            limit = jnp.where(slots[0, e] == slot, 0, limit)
         limits.append(limit)
     bias = jnp.concatenate([bias_of(limits[i], limits[i + 1]) for i in range(0, 24, 2)], axis=1)
     head = lax.broadcasted_iota(jnp.int32, (128, 128), 0)
@@ -281,7 +297,7 @@
         flat[kind, 4] = jnp.where(entry < 32, hi, jnp.where(entry < 64, mid, low))
 
     def spread(kind):
-        for k in range(8):
+        for k in RING + (0,):
             block = (Y + k) % 8
             rows = []
             for p in range(2):
@@ -317,12 +333,13 @@
     loaded(0)
     partial(0, q, [(kv[...].reshape(1536, 576), bias), (kn[...], bias_n)])
 
+    spread(0)
+
     landed(qf.at[q_rows(t)], q_ss.at[0], q_rs.at[0])
     region = qf.at[q_rows(t)]
     for k in range(1, 4):
         send(region, region, q_ss.at[k], q_rs.at[k], dev(Y, zc, (t + k) % 4))
-    spread(0)
-    drain(1)
+    drain(8)
     bounds = qf[q_rows(t), 512:640].astype(F32)[0:1, :]
     spot = inside.astype(F32)
     bias_x = jnp.concatenate(
@@ -339,9 +356,10 @@
     loaded(6)
     for k in range(1, 4):
         landed(qf.at[q_rows((t - k + 4) % 4)], q_ss.at[k], q_rs.at[k])
+
     partial(1, qf[:, 0:576], [(kx[...].reshape(256, 576), bias_x)])
     spread(1)
-    drain(3 + 7)
+    drain(3)
 
     def arrived(kind, j, i):
         def wait():
@@ -352,21 +370,30 @@
         else:
             wait()
 
-    for kind in range(2):
-        for j in range(2):
-            for i in range(4):
-                arrived(kind, j, i)
+    def joined(parts):
+        best = functools.reduce(jnp.maximum, [part[0] for part in parts])
+        shares = [jnp.exp(part[0] - best) for part in parts]
+        norm = functools.reduce(jnp.add, [part[1] * w for part, w in zip(parts, shares)])
+        mixed = functools.reduce(jnp.add, [part[2] * w for part, w in zip(parts, shares)])
+        return best, norm, mixed
+
+    def parts_of(kind, j):
+        found = []
+        for i in range(4):
+            part = l1r[kind, j, i].astype(F32)
+            lse = part[:, 512:513] + part[:, 544:545] + part[:, 576:577]
+            found.append((lse, 1.0, part[:, :LAT]))
+        return found
+
     for j in range(2):
-        parts = [
-            l1r[kind, j ^ kind, i].astype(F32) for kind in range(2) for i in range(4)
-        ]
-        lses = [part[:, 512:513] + part[:, 544:545] + part[:, 576:577] for part in parts]
-        best = functools.reduce(jnp.maximum, lses)
-        shares = [jnp.exp(value - best) for value in lses]
-        norm = functools.reduce(jnp.add, shares)
-        mixed = functools.reduce(
-            jnp.add, [part[:, :LAT] * share for part, share in zip(parts, shares)]
-        )
+        for i in range(4):
+            arrived(0, j, i)
+    early = [joined(parts_of(0, j)) for j in range(2)]
+    for j in range(2):
+        for i in range(4):
+            arrived(1, j, i)
+    for j in range(2):
+        _, norm, mixed = joined([early[j]] + parts_of(1, 1 - j))
         mixed = mixed / norm
         for p in range(2):
             for n in range(4):
@@ -374,19 +401,8 @@
                     p * 8 : p * 8 + 8, n * 128 : (n + 1) * 128
                 ]
 
-    def z_slot(zc_):
-        return (zc_ % 2) * 8 + zc_ // 2
-
-    for k in range(1, 16):
-        to = (zc + k) % 16
-        send(
-            zb.at[to % 2, pl.ds(pl.multiple_of((to // 2) * 8, 8), 8)],
-            zr.at[z_slot(zc)],
-            lz_ss.at[k],
-            lz_rs.at[k],
-            dev(Y, to, t),
-        )
-    zr[z_slot(zc)] = zb[c, pl.ds(pl.multiple_of(z * 8, 8), 8), :]
+    halves = remote(zb.at[sib], zs, lz_ss.at[0], lz_rs.at[0], sibling)
+    halves.start()
     drain(7)
 
     @pl.when(t != 0)
@@ -394,75 +410,77 @@
         to_zero(0).wait_send()
         to_zero(1).wait_send()
 
+    own_half = zb[c]
+    halves.wait_recv()
+    sib_half = zs[...]
+    lower = jnp.where(c == 0, own_half, sib_half)
+    upper = jnp.where(c == 0, sib_half, own_half)
+    for a in range(8):
+        rows = slice(a * 8, a * 8 + 8)
+        zt[a] = jnp.concatenate([lower[rows], upper[rows]], axis=0).astype(BF)
+    for k in RING:
+        to = (z + k) % 8
+        send(zt.at[to], lx.at[t, z], lz_ss.at[k], lz_rs.at[k], dev(Y, to * 2 + c, t))
+    lx[t, z] = zt[z]
+    halves.wait_send()
     loaded(2)
     loaded(3)
     loaded(4)
     loaded(5)
-    for k in range(1, 16):
-        landed(zr.at[z_slot((zc - k + 16) % 16)], lz_ss.at[k], lz_rs.at[k])
-    lx[t] = zr[...].reshape(128, 128).astype(BF)
+    for k in range(1, 8):
+        landed(lx.at[t, (z - k + 8) % 8], lz_ss.at[k], lz_rs.at[k])
     for k in range(1, 4):
         send(lx.at[t], lx.at[t], lx_ss.at[k], lx_rs.at[k], dev(Y, zc, (t + k) % 4))
-    drain(15)
+    drain(7)
     for k in range(4):
         source = (t - k + 4) % 4
         if k:
             landed(lx.at[source], lx_ss.at[k], lx_rs.at[k])
-        un[k] = lx[source].astype(F32)
+        un[k] = lx[source].reshape(128, 128).astype(F32)
         for j in range(2):
             y_from = (Y - source - 4 * j + 8) % 8
             for p in range(2):
                 for n in range(2):
                     for core in range(2):
-                        rows = un[k, pl.ds(core * 64 + j * 4 + p * 2 + n, 8, stride=8), :]
+                        rows = un[k, pl.ds(core * 8 + j * 4 + p * 2 + n, 8, stride=16), :]
                         af[0, n, pl.ds(core * 128 + p * 8 + y_from, 8, stride=16), :] = rows
                         at = pl.multiple_of(core * 128 + y_from * 16 + p * 8, 8)
                         af[1, n, pl.ds(at, 8), :] = rows
     a1[...] = jnp.concatenate([af[0, 0], af[0, 1]], axis=1).astype(BF)
     a2[...] = jnp.concatenate([af[1, 0], af[1, 1]], axis=1).astype(BF)
     drain(3)
-    def reduced(u, operands, weight):
-        before = len(opened)
-        started = []
+    def core_copy(u, s):
+        return remote(
+            core_send.at[u, s], core_recv.at[u, s], core_ss.at[u, s], core_rs.at[u, s], sibling
+        )
+
+    def first_copy(u, s, k):
+        block = (here[s] + k) % 8
+        return remote(
+            send1.at[u, s, pl.ds(pl.multiple_of(block * 16, 16), 16)],
+            recv1.at[u, s, k],
+            p1_ss.at[u, s, k],
+            p1_rs.at[u, s, k],
+            along(s, True, k),
+        )
+
+    def start_first(u):
         for s in range(2):
-            columns = slice(s * HALF, (s + 1) * HALF)
-            rows = pl.ds(pl.multiple_of(sib * 128, 128), 128)
-            core_send[u, s] = dot(operands[s][rows, :], weight[:, columns]).astype(BF)
-            copy = send(
-                core_send.at[u, s],
-                core_recv.at[u, s],
-                core_ss.at[u, s],
-                core_rs.at[u, s],
-                sibling,
-            )
-            started.append(copy)
+            core_copy(u, s).wait_recv()
+            total = tot[s] + core_recv[u, s].astype(F32)
+            tot[s] = total
+            send1[u, s] = total.astype(BF)
+            for k in RING:
+                first_copy(u, s, k).start()
+
+    def rest(u):
         for s in range(2):
-            columns = slice(s * HALF, (s + 1) * HALF)
-            rows = pl.ds(pl.multiple_of(c * 128, 128), 128)
-            tot[s] = dot(operands[s][rows, :], weight[:, columns])
-        first = []
-        for s in range(2):
-            started[s].wait_recv()
-            tot[s] = tot[s] + core_recv[u, s].astype(F32)
-            send1[u, s] = tot[s].astype(BF)
-            copies = []
-            for k in range(1, 8):
-                block = (here[s] + k) % 8
-                copy = send(
-                    send1.at[u, s, pl.ds(pl.multiple_of(block * 16, 16), 16)],
-                    recv1.at[u, s, k],
-                    p1_ss.at[u, s, k],
-                    p1_rs.at[u, s, k],
-                    along(s, True, k),
-                )
-                copies.append(copy)
-            first.append(copies)
-        drain(before + 2)
+            core_copy(u, s).wait_send()
         second = []
         for s in range(2):
             part = tot[s, pl.ds(pl.multiple_of(here[s] * 16, 16), 16), :]
             for k in range(1, 8):
-                first[s][k - 1].wait_recv()
+                first_copy(u, s, k).wait_recv()
                 part = part + recv1[u, s, k].astype(F32)
             for p in range(2):
                 for k in range(PAIRS):
@@ -471,8 +489,8 @@
                     ]
                 pack[s, pl.ds(p * 8 + PAIRS, 8, stride=16), :] = jnp.zeros((8, 128), F32)
             send2[u, s] = pack[s].astype(BF)
-            copies = []
-            for k in range(1, 8):
+            copies = {}
+            for k in RING:
                 block = (there[s] + k) % 8
                 copy = send(
                     send2.at[u, s, pl.ds(pl.multiple_of(block * 16, 16), 16)],
@@ -481,19 +499,31 @@
                     p2_rs.at[u, s, k],
                     along(s, False, k),
                 )
-                copies.append(copy)
+                copies[k] = copy
             second.append(copies)
-        drain(14)
+        for s in range(2):
+            for k in range(1, 8):
+                first_copy(u, s, k).wait_send()
         result = []
         for s in range(2):
             part = pack[s, pl.ds(pl.multiple_of(there[s] * 16, 16), 16), :]
             for k in range(1, 8):
-                second[s][k - 1].wait_recv()
+                second[s][k].wait_recv()
                 part = part + recv2[u, s, k].astype(F32)
             result.append(part)
         return result
 
-    attended = reduced(0, (a1, a2), wov)
+    for s in range(2):
+        columns = slice(s * HALF, (s + 1) * HALF)
+        rows = pl.ds(pl.multiple_of(sib * 128, 128), 128)
+        core_send[0, s] = dot((a1, a2)[s][rows, :], wov[:, columns]).astype(BF)
+        core_copy(0, s).start()
+    for s in range(2):
+        columns = slice(s * HALF, (s + 1) * HALF)
+        rows = pl.ds(pl.multiple_of(c * 128, 128), 128)
+        tot[s] = dot((a1, a2)[s][rows, :], wov[:, columns])
+    start_first(0)
+    attended = rest(0)
 
     sums = []
     squares = []
@@ -521,7 +551,7 @@
             value = jnp.where(row % 8 == 7, square, value)
         region = recv3.at[s, pack_rows(there[s])]
         recv3[s, pack_rows(there[s]), :] = value.astype(BF)
-        for k in range(1, 8):
+        for k in RING:
             send(region, region, p3_ss.at[s, k], p3_rs.at[s, k], along(s, False, k))
     drain(14)
 
@@ -545,11 +575,11 @@
         ]
         normed[s][n_rows(c, here[s]), :] = jnp.concatenate(rows, axis=0).astype(BF)
         region = normed[s].at[n_rows(c, here[s])]
-        for k in range(1, 8):
+        for k in RING:
             send(region, region, p4_ss.at[s, k], p4_rs.at[s, k], along(s, True, k))
         send(region, region, p5_ss.at[s, 0], p5_rs.at[s, 0], sibling)
     drain(14)
-    for k in range(1, 8):
+    for k in (1, 7, 2, 6, 3, 5, 4):
         for s in range(2):
             region = normed[s].at[n_rows(c, (here[s] - k + 8) % 8)]
             landed(region, p4_ss.at[s, k], p4_rs.at[s, k])
@@ -560,50 +590,86 @@
                 normed[s].at[n_rows(sib, (here[s] - k + 8) % 8)], p5_ss.at[s, k], p5_rs.at[s, k]
             )
 
-    part = dot_nt(n0[:, 0:HALF], wc[:, 0:HALF])
-    other = dot_nt(n1[...], wc[:, HALF : 2 * HALF])
-    nothing = jnp.zeros((256, 96), F32)
-    part = jnp.concatenate([part, nothing], axis=1)
-    part = part + swap_rows(jnp.concatenate([other, nothing], axis=1), perm)
-    at = lax.broadcasted_iota(jnp.int32, (256, 128), 1)
-    extra = part[:, 256:384]
-    extra = jnp.where(at == 32, n0[:, HALF : HALF + 1].astype(F32), extra)
-    extra = jnp.where(at == 33, n0[:, HALF + 64 : HALF + 65].astype(F32), extra)
-    gs[:, 0:256] = part[:, 0:256].astype(BF)
-    gs[:, 256:384] = extra.astype(BF)
-
-    def quarter(index):
-        return pl.ds(pl.multiple_of(index * 64, 64), 64)
-
-    gx = []
-    for k in range(1, 4):
-        to = (t + k) % 4
-        gx.append(send(gs.at[quarter(to)], recvx.at[k], gx_ss.at[k], gx_rs.at[k], dev(Y, zc, to)))
+    nothing = jnp.zeros((128, 96), F32)
+    at = lax.broadcasted_iota(jnp.int32, (128, 128), 1)
+    column = lax.broadcasted_iota(jnp.int32, (32, 256), 1)
+
+    def quarter(core, index):
+        return pl.ds(pl.multiple_of(core * 128 + index * 32, 32), 32)
+
+    def products(core):
+        rows = slice(core * 128, (core + 1) * 128)
+        part = jnp.concatenate([dot_nt(n0[rows, 0:HALF], wc[:, 0:HALF]), nothing], axis=1)
+        other = jnp.concatenate([dot_nt(n1[rows, :], wc[:, HALF : 2 * HALF]), nothing], axis=1)
+        part = part + swap_rows(other, perm, core)
+        extra = part[:, 256:384]
+        extra = jnp.where(at == 32, n0[rows, HALF : HALF + 1].astype(F32), extra)
+        extra = jnp.where(at == 33, n0[rows, HALF + 64 : HALF + 65].astype(F32), extra)
+        gs[rows, 0:256] = part[:, 0:256].astype(BF)
+        gs[rows, 256:384] = extra.astype(BF)
+        for k in range(1, 4):
+            to = (t + k) % 4
+            send(
+                gs.at[quarter(core, to)],
+                recvx.at[core, k],
+                gx_ss.at[core, k],
+                gx_rs.at[core, k],
+                dev(Y, zc, to),
+            )
+
+    def gates(core):
+        value = gs[quarter(core, t), :].astype(F32)
+        for k in range(1, 4):
+            landed(recvx.at[core, k], gx_ss.at[core, k], gx_rs.at[core, k])
+            value = value + recvx[core, k].astype(F32)
+        tail = value[:, 256:384]
+        factor = lax.rsqrt((tail[:, 32:33] + tail[:, 33:34]) / D + EPS)
+        gate = value[:, 0:256] * factor
+        up = pltpu.roll(value, 240, 1)[:, 0:256] * factor
+        done = jnp.where(column < 144, gate / (1.0 + jnp.exp(-gate)) * up, 0.0)
+        hid[quarter(core, t), :] = done.astype(BF)
+        region = hid.at[quarter(core, t)]
+        for k in range(1, 4):
+            send(region, region, hx_ss.at[core, k], hx_rs.at[core, k], dev(Y, zc, (t + k) % 4))
+
+    def down(core):
+        for k in range(1, 4):
+            landed(
+                hid.at[quarter(core, (t - k + 4) % 4)], hx_ss.at[core, k], hx_rs.at[core, k]
+            )
+        rows = hid[core * 128 : (core + 1) * 128, :]
+        turned = swap_rows(rows.astype(F32), perm, core).astype(BF)
+        for s in range(2):
+            term = dot((rows, turned)[s], wd[:, s * HALF : (s + 1) * HALF])
+
+            @pl.when(c == core)
+            def _():
+                tot[s] = term
+
+            @pl.when(c != core)
+            def _():
+                core_send[1, s] = term.astype(BF)
+                core_copy(1, s).start()
+
+    products(0)
+    products(1)
     drain(30)
-    value = gs[quarter(t), :].astype(F32)
-    for k in range(1, 4):
-        gx[k - 1].wait_recv()
-        value = value + recvx[k].astype(F32)
-    tail = value[:, 256:384]
-    factor = lax.rsqrt((tail[:, 32:33] + tail[:, 33:34]) / D + EPS)
-    ups = pltpu.roll(value, 240, 1)
-
-    def gated(gate, up):
-        gate = gate * factor
-        return gate / (1.0 + jnp.exp(-gate)) * (up * factor)
-
-    column = lax.broadcasted_iota(jnp.int32, (64, 256), 1)
-    hid[quarter(t), :] = jnp.where(column < 144, gated(value[:, 0:256], ups[:, 0:256]), 0.0).astype(BF)
-    region = hid.at[quarter(t)]
-    for k in range(1, 4):
-        send(region, region, hx_ss.at[k], hx_rs.at[k], dev(Y, zc, (t + k) % 4))
-    drain(3)
-    for k in range(1, 4):
-        landed(hid.at[quarter((t - k + 4) % 4)], hx_ss.at[k], hx_rs.at[k])
-    a2[...] = swap_rows(hid[...].astype(F32), perm).astype(BF)
-    drain(3)
-
-    projected = reduced(1, (hid, a2), wd)
+    gates(0)
+    gates(1)
+    down(0)
+
+    @pl.when(c == 0)
+    def _():
+        start_first(1)
+
+    down(1)
+
+    @pl.when(c == 1)
+    def _():
+        start_first(1)
+
+    drain(12)
+    projected = rest(1)
     for s in range(2):
         value = rsd[s] + projected[s]
         for p in range(2):
@@ -634,8 +700,9 @@
         pltpu.VMEM((2, 8, 16, 640), BF),
         pltpu.VMEM((2, 2, 4, 16, 640), BF),
         pltpu.VMEM((2, 64, 128), F32),
-        pltpu.VMEM((16, 8, 128), F32),
-        pltpu.VMEM((4, 128, 128), BF),
+        pltpu.VMEM((64, 128), F32),
+        pltpu.VMEM((8, 16, 128), BF),
+        pltpu.VMEM((4, 8, 16, 128), BF),
         pltpu.VMEM((4, 128, 128), F32),
         pltpu.VMEM((2, 2, 256, 128), F32),
         pltpu.VMEM((256, 256), BF),
@@ -656,19 +723,23 @@
         pltpu.VMEM((256, HALF + 128), BF),
         pltpu.VMEM((256, HALF), BF),
         pltpu.VMEM((256, 384), BF),
-        pltpu.VMEM((4, 64, 384), BF),
+        pltpu.VMEM((2, 4, 32, 384), BF),
         pltpu.VMEM((256, 256), BF),
         pltpu.VMEM((2, 5, 128, 128), F32),
-        pltpu.SMEM((1,), jnp.int32),
-        dma((8,)),
+        pltpu.SMEM((1, 24), jnp.int32),
+        pltpu.SMEM((1, 4), jnp.int32),
+        pltpu.VMEM((1, 2, 576), BF),
+        pltpu.VMEM((1, 2, 1792), BF),
+        pltpu.VMEM((14, 128), F32),
+        dma((12,)),
         dma((4,)),
         dma((4,)),
         dma((2, 8)),
         dma((2, 2, 4)),
         dma((4,)),
         dma((4,)),
-        dma((16,)),
-        dma((16,)),
+        dma((8,)),
+        dma((8,)),
         dma((2, 2)),
         dma((2, 2)),
         dma((2, 2, 8)),
@@ -681,15 +752,15 @@
         dma((2, 8)),
         dma((2, 8)),
         dma((2, 8)),
-        dma((4,)),
-        dma((4,)),
-        dma((4,)),
-        dma((4,)),
+        dma((2, 4)),
+        dma((2, 4)),
+        dma((2, 4)),
+        dma((2, 4)),
     ]
     return pl.pallas_call(
         kernel,
         out_shape=jax.ShapeDtypeStruct((1, 2, 1792), BF),
-        in_specs=[pl.BlockSpec(memory_space=pltpu.HBM), smem, smem, vmem, vmem, vmem] + [hbm] * 7,
+        in_specs=[smem] + [hbm] * 12,
         out_specs=vmem,
         scratch_shapes=scratch,
         compiler_params=pltpu.CompilerParams(
@@ -699,7 +770,7 @@
             flops=2_000_000_000, bytes_accessed=6_000_000, transcendentals=250_000
         ),
     )(
-        lengths,
+        lengths.reshape(1, 1),
         table,
         slot_of,
         new_kv,

time: 102 us -> 95.6 us (0.937)
  Pallas kernels: 99.5 us -> 93.4 us
    pallas_call x1, Pallas kernels: 99.5 us -> 93.4 us  [body(): pl.pallas_call(kernel, out_shape=jax.ShapeDtypeStruct((1, 2, 1792), BF),...]
where the time goes in v3:
time: 95.6 us; the launch traced here: 95.4 us
  Pallas kernels  93.4 us (98%)
  local copies, waits for them, and re-layouts  1.29 us (1%)
    pallas_call x1, Pallas kernels, body(): pl.pallas_call(kernel, out_shape=jax.ShapeDtypeStruct((1, 2, 1792), BF),...  93.4 us

profile of v3, /device:TPU:1, one launch (start us, length us, event | category | flops | bytes accessed | tf_op | source)
XLA Modules:
  0.0 95.4 jit_solution(4318729004429850343)
XLA Ops:
  0.7 93.4 %shard_map.127 = bf16[1,2,1792]{2,1,0:T(2,128)(2,1)} custom-call(s32[1,1]{1,0:T(1,128)} %bitcast.4.lengths_ref, s32[1,24]{1,0:T(1,128)} %table_ref.1, s32[1,4]{1,0:T(1,128)} %slot_ref.1, bf16[1,2,576]{2,1,0:T(2,128)(2,1)} %new_ref.1, bf16[1,2,1792]{2,1,0:T(2,128)(2,1)} %resid_ref.1, f32[14,128]{1,0:T(8,128)} %bitcast.7, bf16[1,24,64,576]{3,2,1,0:T(8,128)(2,1)} %cache_ref.1, ...), custom_call_target="tpu_custom_call" | custom-call | flops 2000000000 | bytes 6000000 | tf_op jit(solution)/shard_map/pallas_call | solution.py:760
  94.1 1.3 %copy.16 = bf16[1,2,1792]{2,1,0:T(2,128)(2,1)} copy(bf16[1,2,1792]{2,1,0:T(2,128)(2,1)} %shard_map.127) | data formatting | bytes 14336

commit v4 on v3

--- a/solution.py
+++ b/solution.py
@@ -20,7 +20,9 @@
 PAIRS = 7
 
 NT = (((1,), (1,)), ((), ()))
+ROUND = (2, 1, 3)
 RING = (4, 3, 5, 2, 6, 1, 7)
+TURNS = RING + (0,)
 
 
 def dot(a, b):
@@ -102,6 +104,7 @@
     newest,
     base,
     gains,
+    count,
     load_sem,
     q_ss,
     q_rs,
@@ -182,20 +185,13 @@
         pltpu.make_async_copy(new_ref, newest, load_sem.at[9]),
         pltpu.make_async_copy(resid_ref, base, load_sem.at[10]),
         pltpu.make_async_copy(gain_ref, gains, load_sem.at[11]),
+        pltpu.make_async_copy(lengths_ref, count, load_sem.at[12]),
     ]
-    for load in loads:
-        load.start()
 
     waiting = dict(enumerate(loads))
 
     def loaded(n):
         waiting.pop(n).wait()
-
-    def finish():
-        drain(len(opened))
-        for load in waiting.values():
-            load.wait()
-        out_ref[...] = jnp.zeros((1, 2, 1792), BF)
 
     barrier = pltpu.get_barrier_semaphore()
     for k in RING:
@@ -217,12 +213,15 @@
         to = dev(Y, ((z + k) % 8) * 2 + c, t)
         pl.semaphore_signal(barrier, inc=1, device_id=to, device_id_type=MESH)
     pl.semaphore_signal(barrier, inc=1, device_id=sibling, device_id_type=MESH)
+    for n in (1, 7, 8, 12):
+        loads[n].start()
     pl.semaphore_wait(barrier, jnp.where(t == 0, 25, 26))
 
     lane = lax.broadcasted_iota(jnp.int32, (1, 128), 1)
     loaded(7)
     loaded(8)
-    length = lengths_ref[0, 0]
+    loaded(12)
+    length = count[0, 0]
     late = [length - numbers[0, slots[0, e]] * 64 for e in range(4)]
     within = jnp.zeros((1, 128), jnp.int32)
     for e in range(4):
@@ -241,6 +240,9 @@
     first_q = send(
         qx.at[q_rows(t)], qf.at[q_rows(t)], q_ss.at[0], q_rs.at[0], dev((Y + 4) % 8, zc, t)
     )
+
+    for n in (0, 6, 9, 10, 11, 2, 3, 4, 5):
+        loads[n].start()
 
     loaded(9)
     loaded(10)
@@ -337,7 +339,7 @@
 
     landed(qf.at[q_rows(t)], q_ss.at[0], q_rs.at[0])
     region = qf.at[q_rows(t)]
-    for k in range(1, 4):
+    for k in ROUND:
         send(region, region, q_ss.at[k], q_rs.at[k], dev(Y, zc, (t + k) % 4))
     drain(8)
     bounds = qf[q_rows(t), 512:640].astype(F32)[0:1, :]
@@ -429,7 +431,7 @@
     loaded(5)
     for k in range(1, 8):
         landed(lx.at[t, (z - k + 8) % 8], lz_ss.at[k], lz_rs.at[k])
-    for k in range(1, 4):
+    for k in ROUND:
         send(lx.at[t], lx.at[t], lx_ss.at[k], lx_rs.at[k], dev(Y, zc, (t + k) % 4))
     drain(7)
     for k in range(4):
@@ -449,36 +451,51 @@
     a1[...] = jnp.concatenate([af[0, 0], af[0, 1]], axis=1).astype(BF)
     a2[...] = jnp.concatenate([af[1, 0], af[1, 1]], axis=1).astype(BF)
     drain(3)
-    def core_copy(u, s):
+    def core_copy(u, s, part):
+        region = (u, s, pl.ds(part * 64, 64))
         return remote(
-            core_send.at[u, s], core_recv.at[u, s], core_ss.at[u, s], core_rs.at[u, s], sibling
+            core_send.at[region],
+            core_recv.at[region],
+            core_ss.at[u, s, part],
+            core_rs.at[u, s, part],
+            sibling,
         )
 
     def first_copy(u, s, k):
-        block = (here[s] + k) % 8
         return remote(
-            send1.at[u, s, pl.ds(pl.multiple_of(block * 16, 16), 16)],
+            send1.at[u, s, pl.ds(TURNS.index(k) * 16, 16)],
             recv1.at[u, s, k],
             p1_ss.at[u, s, k],
             p1_rs.at[u, s, k],
             along(s, True, k),
         )
 
+    def half_rows(source, s, core, part):
+        blocks = []
+        for k in TURNS[part * 4 : part * 4 + 4]:
+            at = pl.multiple_of(core * 128 + ((here[s] + k) % 8) * 16, 16)
+            blocks.append(source[pl.ds(at, 16), :])
+        return jnp.concatenate(blocks, axis=0)
+
     def start_first(u):
-        for s in range(2):
-            core_copy(u, s).wait_recv()
-            total = tot[s] + core_recv[u, s].astype(F32)
-            tot[s] = total
-            send1[u, s] = total.astype(BF)
-            for k in RING:
-                first_copy(u, s, k).start()
+        for part in range(2):
+            rows = slice(part * 64, part * 64 + 64)
+            for s in range(2):
+                core_copy(u, s, part).wait_recv()
+                total = tot[s, rows, :] + core_recv[u, s, rows, :].astype(F32)
+                tot[s, rows, :] = total
+                send1[u, s, rows, :] = total.astype(BF)
+                for k in TURNS[part * 4 : part * 4 + 4]:
+                    if k:
+                        first_copy(u, s, k).start()
 
     def rest(u):
         for s in range(2):
-            core_copy(u, s).wait_send()
+            for part in range(2):
+                core_copy(u, s, part).wait_send()
         second = []
         for s in range(2):
-            part = tot[s, pl.ds(pl.multiple_of(here[s] * 16, 16), 16), :]
+            part = tot[s, 112:128, :]
             for k in range(1, 8):
                 first_copy(u, s, k).wait_recv()
                 part = part + recv1[u, s, k].astype(F32)
@@ -513,15 +530,17 @@
             result.append(part)
         return result
 
+    for part in range(2):
+        for s in range(2):
+            rows = slice(part * 64, part * 64 + 64)
+            columns = slice(s * HALF, (s + 1) * HALF)
+            term = dot(half_rows((a1, a2)[s], s, sib, part), wov[:, columns])
+            core_send[0, s, rows, :] = term.astype(BF)
+            core_copy(0, s, part).start()
     for s in range(2):
         columns = slice(s * HALF, (s + 1) * HALF)
-        rows = pl.ds(pl.multiple_of(sib * 128, 128), 128)
-        core_send[0, s] = dot((a1, a2)[s][rows, :], wov[:, columns]).astype(BF)
-        core_copy(0, s).start()
-    for s in range(2):
-        columns = slice(s * HALF, (s + 1) * HALF)
-        rows = pl.ds(pl.multiple_of(c * 128, 128), 128)
-        tot[s] = dot((a1, a2)[s][rows, :], wov[:, columns])
+        whole = [half_rows((a1, a2)[s], s, c, part) for part in range(2)]
+        tot[s] = dot(jnp.concatenate(whole, axis=0), wov[:, columns])
     start_first(0)
     attended = rest(0)
 
@@ -607,7 +626,7 @@
         extra = jnp.where(at == 33, n0[rows, HALF + 64 : HALF + 65].astype(F32), extra)
         gs[rows, 0:256] = part[:, 0:256].astype(BF)
         gs[rows, 256:384] = extra.astype(BF)
-        for k in range(1, 4):
+        for k in ROUND:
             to = (t + k) % 4
             send(
                 gs.at[quarter(core, to)],
@@ -629,7 +648,7 @@
         done = jnp.where(column < 144, gate / (1.0 + jnp.exp(-gate)) * up, 0.0)
         hid[quarter(core, t), :] = done.astype(BF)
         region = hid.at[quarter(core, t)]
-        for k in range(1, 4):
+        for k in ROUND:
             send(region, region, hx_ss.at[core, k], hx_rs.at[core, k], dev(Y, zc, (t + k) % 4))
 
     def down(core):
@@ -638,18 +657,21 @@
                 hid.at[quarter(core, (t - k + 4) % 4)], hx_ss.at[core, k], hx_rs.at[core, k]
             )
         rows = hid[core * 128 : (core + 1) * 128, :]
-        turned = swap_rows(rows.astype(F32), perm, core).astype(BF)
-        for s in range(2):
-            term = dot((rows, turned)[s], wd[:, s * HALF : (s + 1) * HALF])
-
-            @pl.when(c == core)
-            def _():
-                tot[s] = term
-
-            @pl.when(c != core)
-            def _():
-                core_send[1, s] = term.astype(BF)
-                core_copy(1, s).start()
+        a2[core * 128 : (core + 1) * 128, :] = swap_rows(rows.astype(F32), perm, core).astype(BF)
+        for part in range(2):
+            for s in range(2):
+                rows = slice(part * 64, part * 64 + 64)
+                columns = slice(s * HALF, (s + 1) * HALF)
+                term = dot(half_rows((hid, a2)[s], s, core, part), wd[:, columns])
+
+                @pl.when(c == core)
+                def _():
+                    tot[s, rows, :] = term
+
+                @pl.when(c != core)
+                def _():
+                    core_send[1, s, rows, :] = term.astype(BF)
+                    core_copy(1, s, part).start()
 
     products(0)
     products(1)
@@ -683,7 +705,6 @@
 def body(
     cache, sent, slot_of, table, lengths, new_kv, queries, resid, gain, w_ov, w_gate, w_up, w_down
 ):
-    smem = pl.BlockSpec(memory_space=pltpu.SMEM)
     vmem = pl.BlockSpec(memory_space=pltpu.VMEM)
     hbm = pl.BlockSpec(memory_space=pl.ANY)
     dma = pltpu.SemaphoreType.DMA
@@ -731,7 +752,8 @@
         pltpu.VMEM((1, 2, 576), BF),
         pltpu.VMEM((1, 2, 1792), BF),
         pltpu.VMEM((14, 128), F32),
-        dma((12,)),
+        pltpu.SMEM((1, 1), jnp.int32),
+        dma((13,)),
         dma((4,)),
         dma((4,)),
         dma((2, 8)),
@@ -740,8 +762,8 @@
         dma((4,)),
         dma((8,)),
         dma((8,)),
-        dma((2, 2)),
-        dma((2, 2)),
+        dma((2, 2, 2)),
+        dma((2, 2, 2)),
         dma((2, 2, 8)),
         dma((2, 2, 8)),
         dma((2, 2, 8)),
@@ -760,7 +782,7 @@
     return pl.pallas_call(
         kernel,
         out_shape=jax.ShapeDtypeStruct((1, 2, 1792), BF),
-        in_specs=[smem] + [hbm] * 12,
+        in_specs=[hbm] * 13,
         out_specs=vmem,
         scratch_shapes=scratch,
         compiler_params=pltpu.CompilerParams(

time: 95.6 us -> 94.7 us (level)
  no operation moved by 1% of the time
where the time goes in v4:
time: 94.7 us; the launch traced here: 94.5 us
  Pallas kernels  92.6 us (98%)
  local copies, waits for them, and re-layouts  1.29 us (1%)
    pallas_call x1, Pallas kernels, body(): pl.pallas_call(kernel, out_shape=jax.ShapeDtypeStruct((1, 2, 1792), BF),...  92.6 us

profile of v4, /device:TPU:1, one launch (start us, length us, event | category | flops | bytes accessed | tf_op | source)
XLA Modules:
  0.0 94.5 jit_solution(15898012735615431697)
XLA Ops:
  0.7 92.6 %shard_map.127 = bf16[1,2,1792]{2,1,0:T(2,128)(2,1)} custom-call(s32[1,1]{1,0:T(1,128)} %bitcast.4.lengths_ref, s32[1,24]{1,0:T(1,128)} %table_ref.1, s32[1,4]{1,0:T(1,128)} %slot_ref.1, bf16[1,2,576]{2,1,0:T(2,128)(2,1)} %new_ref.1, bf16[1,2,1792]{2,1,0:T(2,128)(2,1)} %resid_ref.1, f32[14,128]{1,0:T(8,128)} %bitcast.7, bf16[1,24,64,576]{3,2,1,0:T(8,128)(2,1)} %cache_ref.1, ...), custom_call_target="tpu_custom_call" | custom-call | flops 2000000000 | bytes 6000000 | tf_op jit(solution)/shard_map/pallas_call | solution.py:782
  93.2 1.3 %copy.16 = bf16[1,2,1792]{2,1,0:T(2,128)(2,1)} copy(bf16[1,2,1792]{2,1,0:T(2,128)(2,1)} %shard_map.127) | data formatting | bytes 14336
